TPU v7x, 32 devices: a whole 2x2x4 slice. The times are simulated.
32 devices in a mesh: dp: 8 (over y, x, core), mp: 4 (over z).
Axes of the slice: x: 2, y: 2, z: 4, core: 2. Of those that a mesh axis runs over, the one named last changes fastest.
Arguments:
- tokens: bfloat16 [384, 256, 384], P(('dp', 'mp')), may hold values from -6 to 6
- segment_ids: int32 [384, 256], P(('dp', 'mp')), may hold values from 0 to 3, never falling along the last dimension, each value on 1 to 160 neighbouring positions
- valid_len: int32 [384], P(('dp', 'mp')), may hold values from 192 to 256
- qkv_weight: bfloat16 [384, 1152], P('dp'), may hold values from -0.3125 to 0.3125
- out_weight: bfloat16 [384, 384], P('dp'), may hold values from -1.25 to 1.25
- up_weight: bfloat16 [384, 1536], P('dp', 'mp'), may hold values from -0.3125 to 0.3125
- down_weight: bfloat16 [384, 1536], P('dp', 'mp'), may hold values from -0.3125 to 0.3125
- conv_weight: bfloat16 [3, 384], P(None, 'dp'), may hold values from -3 to 3
- ln1_gain: bfloat16 [384], P('dp'), may hold values from 0.099609375 to 1.8984375
- ln1_shift: bfloat16 [384], P('dp'), may hold values from -3 to 3
- ln2_gain: bfloat16 [384], P('dp'), may hold values from 0.099609375 to 1.8984375
- ln2_shift: bfloat16 [384], P('dp'), may hold values from -3 to 3
- cotangent: bfloat16 [384, 256, 384], P(('dp', 'mp')), may hold values from -6 to 6
Outputs:
- layer_out: bfloat16 [384, 256, 384], P(('dp', 'mp'))
- input_grad: bfloat16 [384, 256, 384], P(('dp', 'mp'))
- grad_qkv: float32 [384, 1152], P('dp')
- grad_out: float32 [384, 384], P('dp')
- grad_up: float32 [384, 1536], P('dp', 'mp')
- grad_down: float32 [384, 1536], P('dp', 'mp')
- grad_conv: float32 [3, 384], P(None, 'dp')
- grad_ln1_gain: float32 [384], P('dp')
- grad_ln1_shift: float32 [384], P('dp')
- grad_ln2_gain: float32 [384], P('dp')
- grad_ln2_shift: float32 [384], P('dp')
Inputs may be any that keep to these rules, and one draw needn't show every extreme that they name: `segment_ids`: within a row the numbers never fall, so each image is a run of consecutive positions, the longest of 160.
All inputs are finite; a program needn't handle non-finite values.
Results may differ from a plain program's by a relative error of at most 0.02.
Values may be sent and summed in bfloat16 or wider, within the bound.
No kernel may reach another device: no remote copies, remote signals or barrier semaphores. Data moves between devices by JAX's collectives and lax.ppermute only.
A program may use at most 192 MiB of HBM per device.

v0:
```python
import functools
import math

import jax
import jax.numpy as jnp
from jax import lax
from jax.experimental import pallas as pl
from jax.experimental.pallas import tpu as pltpu
from jax.sharding import PartitionSpec as P

HEADS = 6
VECTORS = 128
LANES = 128
BF = jnp.bfloat16
F32 = jnp.float32
MIB = 1024 * 1024
VMEM_LIMITS = dict(forward_attention=32, feed_forward=44, backward=42, layer_output=16)


def mm(lhs, rhs):
    return lax.dot_general(lhs, rhs, (((1,), (0,)), ((), ())), preferred_element_type=F32)


def mm_nt(lhs, rhs):
    return lax.dot_general(lhs, rhs, (((1,), (1,)), ((), ())), preferred_element_type=F32)


def tree_sum(items):
    items = list(items)
    while len(items) > 1:
        items = [a + b for a, b in zip(items[::2], items[1::2])]
    return items[0]


def pack_weights(qkv_ref, up_ref, down_ref, conv_ref, g1_ref, s1_ref, g2_ref, s2_ref, narrow_ref, ff_ref, rows_ref):
    own, ffs = up_ref.shape
    rows_ref[...] = jnp.zeros_like(rows_ref)
    rows_ref[0:3, :own] = conv_ref[...].astype(F32)
    for i, ref in enumerate((g1_ref, s1_ref, g2_ref, s2_ref)):
        rows_ref[3 + i : 4 + i, :own] = ref[...].astype(F32)
    wide = qkv_ref.shape[1]
    narrow_ref[:, :wide] = qkv_ref[...]
    narrow_ref[:, wide:] = rows_ref[...].T[:own].astype(BF)
    ff_ref[:own] = up_ref[...]
    ff_ref[own:] = down_ref[...]


def tiles(total, size):
    return [slice(at, at + size) for at in range(0, total, size)]


def weave(*strands):
    strands = [strand for strand in strands if strand]
    total = sum(len(strand) for strand in strands)
    pieces = [((i + 0.5) / len(strand), j, piece) for j, strand in enumerate(strands) for i, piece in enumerate(strand)]
    assert len(pieces) == total
    for _, _, piece in sorted(pieces, key=lambda item: item[:2]):
        piece()


def twice(tile, lanes):
    return jnp.concatenate([tile] * (lanes // LANES), axis=1)


def load_columns(packed_ref, col_ref, places):
    for i, place in enumerate(places):
        column = packed_ref[:, place : place + 1].astype(F32)
        col_ref[i] = jnp.broadcast_to(column, (column.shape[0], LANES))


def pairwise(items, combine):
    items = list(items)
    while len(items) > 1:
        odd = items[len(items) // 2 * 2 :]
        items = [combine(a, b) for a, b in zip(items[::2], items[1::2])] + odd
    return items[0]


def fold(values, combine=jnp.add):
    return pairwise([values[t] for t in tiles(values.shape[0], 8)], combine)


def column_mean(values):
    return jnp.sum(fold(values), axis=0, keepdims=True) * (1.0 / values.shape[0])


def norm_columns(values):
    centred = values - column_mean(values)
    scale = lax.rsqrt(column_mean(centred * centred) + 1e-06)
    return centred * scale, scale


def fold_lanes(values):
    return sum(values[:, t] for t in tiles(values.shape[1], LANES))


def forward_attention(index_ref, len_ref, tok_ref, seg_ref, *refs, pieces):
    cores = 2 if pieces > 1 else 1
    piece_refs = refs[:cores]
    (
        five_ref, mc_ref, v_ref, e_ref, facts_ref, packed_ref, w_ref,
        wt_ref, wide_ref, col_ref, key_mask_ref, query_mask_ref, key_ref, value_ref,
    ) = refs[cores:]
    x_ref, norm_ref, q_ref, k_ref, att_ref = [five_ref.at[:, i] for i in range(5)]
    aux_ref, inv_ref = facts_ref.at[:, :8], facts_ref.at[:, 8:]
    rows, seq, width = tok_ref.shape
    head = width // HEADS
    step = pl.program_id(0)

    @pl.when(step == 0)
    def _():
        own = width // pieces
        for i in range(pieces):
            here = pl.ds(pl.multiple_of(index_ref[i] * own, 16), own)
            wide_ref[here, :] = piece_refs[i % cores][i // cores * own : (i // cores + 1) * own]
        w_ref[...] = wide_ref[:, : 3 * width]
        wt_ref[...] = wide_ref[:, : 3 * width].T
        packed_ref[...] = wide_ref[:, 3 * width :]
        load_columns(packed_ref, col_ref, range(5))
        col_ref[1] = col_ref[1] + 1.0

    place = lax.broadcasted_iota(jnp.int32, (1, seq), 1)
    zero = jnp.zeros((head, seq), BF)

    def preparation(r):
        known = {}

        def start():
            segs = seg_ref[pl.ds(step * rows + r, 1), :].astype(F32)
            valid = place < len_ref[step * rows + r]
            number = jnp.where(valid, segs, -1.0)
            links = jnp.where(valid & (place > 0) & (number == pltpu.roll(number, 1, 1)), 1.0, 0.0)
            next_links = jnp.where(place < seq - 1, pltpu.roll(links, seq - 1, 1), 0.0)
            none = jnp.zeros_like(links)
            aux = jnp.concatenate([links, next_links, number, none, none, none, none, none], axis=0)
            aux_ref[r] = aux
            x_ref[r] = tok_ref[r].T
            known.update(segs=segs, links=links, next_links=next_links, key_number=aux.T[:, 2:3])

        def mask():
            number = known["key_number"]
            lane = lax.broadcasted_iota(jnp.int32, (seq, LANES), 1)
            itself = lax.broadcasted_iota(jnp.int32, (seq, LANES), 0) - (seq - LANES)
            chosen = (lane.astype(F32) == number) | ((number < 0.0) & (lane == itself))
            key_mask_ref[r] = jnp.where(chosen, 1.0, 0.0).astype(BF)
            slot = lax.broadcasted_iota(jnp.int32, (LANES, seq), 0)
            itself = lax.broadcasted_iota(jnp.int32, (LANES, seq), 1) - (seq - LANES)
            open_to = (slot.astype(F32) == known["segs"]) | ((slot >= LANES // 2) & (slot == itself))
            query_mask_ref[r] = jnp.where(open_to, 0.0, -1e30).astype(BF)

        def conv(t):
            base = x_ref[r, t].astype(F32)
            before = pltpu.roll(base, 1, 1) * known["links"]
            after = pltpu.roll(base, seq - 1, 1) * known["next_links"]
            conv0, conv1, conv2 = [twice(col_ref[i, t], seq) for i in range(3)]
            mc_ref[r, t] = before * conv0 + base * conv1 + after * conv2

        def norm(t):
            n, _ = norm_columns(mc_ref[r, :, t])
            norm_ref[r, :, t] = (n * col_ref[3] + col_ref[4]).astype(BF)

        pieces = [start] + [functools.partial(conv, t) for t in tiles(width, 32)]
        pieces += [functools.partial(norm, t) for t in tiles(seq, LANES)]
        return pieces + [mask]

    def project():
        normed = jnp.concatenate([norm_ref[r] for r in range(rows)], axis=1)
        for i, ref in enumerate((q_ref, k_ref, value_ref)):
            part = mm(wt_ref[i * width : (i + 1) * width], normed)
            part = (part * (head ** (-0.5) * math.log2(math.e)) if i == 0 else part).astype(BF)
            for r in range(rows):
                ref[r] = part[:, r * seq : (r + 1) * seq]
        for r in range(rows):
            key_ref[r] = k_ref[r].T
            v_ref[r] = value_ref[r].T

    def scores(r, p):
        low, high = [q_ref[r, h * head : (h + 1) * head] for h in (2 * p, 2 * p + 1)]
        both = jnp.concatenate([jnp.concatenate([low, zero], axis=1), jnp.concatenate([zero, high], axis=1)], axis=0)
        keys = jnp.concatenate([key_ref[r, :, 2 * p * head : 2 * (p + 1) * head], key_mask_ref[r]], axis=1)
        masks = jnp.concatenate([query_mask_ref[r], query_mask_ref[r]], axis=1)
        return mm(keys, jnp.concatenate([both, masks], axis=0))

    def attended(r, p):
        both = jnp.concatenate([e_ref[r, 2 * p], e_ref[r, 2 * p + 1]], axis=1)
        product = mm(value_ref[r, 2 * p * head : 2 * (p + 1) * head], both)
        parts = []
        for i in range(2):
            att = product[i * head : (i + 1) * head, i * seq : (i + 1) * seq] * inv_ref[r, 2 * p + i : 2 * p + i + 1]
            parts.append(att.astype(BF))
        return jnp.concatenate(parts, axis=0)

    def soften(r, p, product):
        for i in range(2):
            for t in tiles(seq, LANES):
                masked = product[:, i * seq + t.start : i * seq + t.stop]
                raised = jnp.exp2(masked - jnp.max(fold(masked, jnp.maximum), axis=0, keepdims=True))
                inv_ref[r, 2 * p + i : 2 * p + i + 1, t] = 1.0 / jnp.sum(fold(raised), axis=0, keepdims=True)
                e_ref[r, 2 * p + i, :, t] = raised.astype(BF)

    weave(*[preparation(r) for r in range(rows)])
    project()
    work = [(r, p) for r in range(rows) for p in range(HEADS // 2)]
    current, last = scores(*work[0]), None
    for at, (r, p) in enumerate(work):
        following = scores(*work[at + 1]) if at + 1 < len(work) else None
        finished = attended(*last) if last else None
        soften(r, p, current)
        if last:
            att_ref[last[0], 2 * last[1] * head : 2 * (last[1] + 1) * head] = finished
        current, last = following, (r, p)
    att_ref[last[0], 2 * last[1] * head : 2 * (last[1] + 1) * head] = attended(*last)


def gelu_parts(y):
    twice_cdf = lax.erf(y) + 1.0
    bell = jnp.exp2(y * y * -math.log2(math.e) + math.log2(2.0 / math.sqrt(math.pi)))
    return y * twice_cdf, twice_cdf + y * bell


def feed_forward(index_ref, five_ref, mc_ref, ct_ref, packed_ref, *refs, pieces, shards):
    att_ref = five_ref.at[:, 0]
    groups = 2 if pieces > 1 else 1
    piece_refs = refs[:groups]
    hidden_out, mixed_out, gm_ref, ga_ref, gs_ref, down_ref = refs[groups : groups + 6]
    gw_refs = refs[groups + 6 : 2 * groups + 6]
    (
        up_ref, upt_ref, downt_ref, out_ref, outt_ref, up_acc, down_acc, out_acc, col_acc, col_ref,
        n_ref, norm_ref, ctt_ref, gp_ref, gn_ref, scale_ref, branch_ref, hidden_ref, mixed_ref, sems,
    ) = refs[2 * groups + 6 :]
    rows, seq, width = ct_ref.shape
    ff = up_ref.shape[1]
    ffs = ff // shards
    own = width // pieces
    step = pl.program_id(0)

    @pl.when(step == 0)
    def _():
        for acc in (up_acc, down_acc, out_acc, col_acc):
            acc[...] = jnp.zeros_like(acc)
        for i in range(pieces):
            here = pl.ds(pl.multiple_of(index_ref[i] * own, 16), own)
            ref, first = piece_refs[i % groups], i // groups * (2 * shards + 1) * own
            for j in range(shards):
                at = first + 2 * j * own
                up_ref[here, j * ffs : (j + 1) * ffs] = ref[at : at + own]
                down_ref[here, j * ffs : (j + 1) * ffs] = ref[at + own : at + 2 * own]
            at = first + 2 * shards * own
            out_ref[here, :] = ref[at : at + own]
        upt_ref[...] = up_ref[...].T
        downt_ref[...] = down_ref[...].T
        outt_ref[...] = out_ref[...].T
        load_columns(packed_ref, col_ref, (5, 6, 5))
        for i, factor in enumerate((0.5, math.sqrt(0.5), math.sqrt(0.5))):
            col_ref[i] = col_ref[i] * factor

    def copies(at, g):
        place = at * pairs + g
        return [
            pltpu.make_async_copy(hidden_ref.at[g], hidden_out.at[place], sems.at[0, g]),
            pltpu.make_async_copy(mixed_ref.at[g], mixed_out.at[place], sems.at[1, g]),
        ]

    pairs = n_ref.shape[0]

    @pl.when(step > 0)
    def _():
        for g in range(pairs):
            for copy in copies(step - 1, g):
                copy.wait()

    def begin(g):
        pair = range(g * paired, (g + 1) * paired)
        attended = jnp.concatenate([att_ref[r] for r in pair], axis=1)
        branch = mm(outt_ref[...], attended)
        for i, r in enumerate(pair):
            lanes = slice(i * seq, (i + 1) * seq)
            ctt_ref[g, :, lanes] = ct_ref[r].T
            mixed_ref[g, :, lanes] = mc_ref[r] + branch[:, lanes]
        for t in spots:
            n, scale = norm_columns(mixed_ref[g, :, t])
            n_ref[g, :, t] = n
            scale_ref[g, 0:1, t] = scale
            norm_ref[g, :, t] = (n * col_ref[2] + col_ref[1]).astype(BF)

    def activate(g, block):
        pre = mm(upt_ref[block], norm_ref[g])
        grad_hidden = mm(downt_ref[block], ctt_ref[g])
        for low in range(0, block.stop - block.start, 16):
            part = slice(low, low + 16)
            here = slice(block.start + low, block.start + low + 16)
            hidden, slope = gelu_parts(pre[part])
            hidden_ref[g, here] = hidden.astype(BF)
            gp_ref[g, here] = (grad_hidden[part] * slope).astype(BF)

    def weigh(g):
        gn_ref[g] = mm(up_ref[...], gp_ref[g])
        down_acc[...] += mm_nt(ctt_ref[g], hidden_ref[g])
        up_acc[...] += mm_nt(norm_ref[g], gp_ref[g])

    def norm_back(g):
        mean_e = [jnp.zeros((8, LANES), F32) for _ in spots]
        mean_en = [jnp.zeros((8, LANES), F32) for _ in spots]
        for d in tiles(width, 32):
            column = col_ref[0, d]
            gain_sum, shift_sum = col_acc[0, d], col_acc[1, d]
            for i, t in enumerate(spots):
                grad_n = gn_ref[g, d, t]
                product = grad_n * n_ref[g, d, t]
                gain_sum += product
                shift_sum += grad_n
                mean_e[i] += fold(grad_n * column)
                mean_en[i] += fold(product * column)
            col_acc[0, d] = gain_sum
            col_acc[1, d] = shift_sum
        for i, t in enumerate(spots):
            me = jnp.sum(mean_e[i], axis=0, keepdims=True) * (1.0 / width)
            men = jnp.sum(mean_en[i], axis=0, keepdims=True) * (1.0 / width)
            row, inside = divmod(t.start, seq)
            for d in tiles(width, 32):
                change = scale_ref[g, 0:1, t] * (gn_ref[g, d, t] * col_ref[0, d] - me - n_ref[g, d, t] * men)
                grad_mixed = ctt_ref[g, d, t].astype(F32) + change
                gm_ref[g * paired + row, d, inside : inside + LANES] = grad_mixed
                branch_ref[g, d, t] = grad_mixed.astype(BF)

    def end(g):
        pair = range(g * paired, (g + 1) * paired)
        attended = jnp.concatenate([att_ref[r] for r in pair], axis=1)
        grad_attended = mm(out_ref[...], branch_ref[g]).astype(BF)
        for i, r in enumerate(pair):
            ga_ref[r] = grad_attended[:, i * seq : (i + 1) * seq]
        out_acc[...] += mm_nt(attended, branch_ref[g])

    paired = rows // pairs
    spots = tiles(paired * seq, LANES)
    begin(0)
    copies(step, 0)[1].start()
    for g in range(pairs):
        for block in tiles(ff, 128):
            activate(g, block)
        copies(step, g)[0].start()
        if g + 1 < pairs:
            begin(g + 1)
            copies(step, g + 1)[1].start()
        weigh(g)
        norm_back(g)
        end(g)

    @pl.when(step == pl.num_programs(0) - 1)
    def _():
        for g in range(pairs):
            for copy in copies(step, g):
                copy.wait()
        for i in range(pieces):
            here = pl.ds(pl.multiple_of(index_ref[i] * own, 16), own)
            place = gw_refs[i % groups]
            for j in range(shards):
                cols = slice(j * ffs, (j + 1) * ffs)
                place[i // groups, :, 2 * j * ffs : (2 * j + 1) * ffs] = (up_acc[here, cols] * math.sqrt(0.5)).astype(BF)
                place[i // groups, :, (2 * j + 1) * ffs : (2 * j + 2) * ffs] = (down_acc[here, cols] * math.sqrt(0.5)).astype(BF)
            place[i // groups, :, 2 * ff :] = out_acc[here, :].astype(BF)
        gs_ref[...] = jnp.zeros_like(gs_ref)
        for i in range(2):
            gs_ref[5 + i : 6 + i] = jnp.sum(col_acc[i].T, axis=0, keepdims=True) * 0.5


def layer_output(hidden_ref, mixed_ref, down_ref, lo_ref):
    rows, seq, _ = lo_ref.shape
    total = (mixed_ref[0] + mm(down_ref[...], hidden_ref[0]) * math.sqrt(0.5)).astype(BF)
    for r in range(rows):
        lo_ref[r] = total[:, r * seq : (r + 1) * seq].T


def backward(
    five_ref, mc_ref, v_ref, e_ref, facts_ref, ga_ref, gm_ref, index_ref, w_ref, packed_ref, other_ref, ig_ref, gs_ref, *refs, pieces,
):
    x_ref, norm_ref, q_ref, k_ref, att_ref = [five_ref.at[:, i] for i in range(5)]
    aux_ref, inv_ref = facts_ref.at[:, :8], facts_ref.at[:, 8:]
    gw_refs = refs[:-11]
    (
        proj_ref, w_acc, norm_cat, soft_ref, logit_ref, gn_ref, acc_ref, col_ref, n_ref, g_ref, turn_ref
    ) = refs[-11:]
    rows, seq, width = v_ref.shape
    own = width // pieces
    head = width // HEADS
    step = pl.program_id(0)

    @pl.when(step == 0)
    def _():
        w_acc[...] = jnp.zeros_like(w_acc)
        acc_ref[...] = jnp.zeros_like(acc_ref)
        load_columns(packed_ref, col_ref, range(4))
        col_ref[1] = col_ref[1] + 1.0

    zero = jnp.zeros((head, seq), BF)
    work = [(r, p) for r in range(rows) for p in range(HEADS // 2)]

    def opening(r, p):
        grads, inners = [], []
        for h in (2 * p, 2 * p + 1):
            part = slice(h * head, (h + 1) * head)
            grad_att = ga_ref[r, part].astype(F32) * inv_ref[r, h : h + 1]
            inners.append(jnp.sum(fold(grad_att * att_ref[r, part].astype(F32)), axis=0, keepdims=True))
            grads.append(grad_att.astype(BF))
        low, high = grads
        both = jnp.concatenate([jnp.concatenate([low, zero], axis=1), jnp.concatenate([zero, high], axis=1)], axis=0)
        product = mm(v_ref[r, :, 2 * p * head : 2 * (p + 1) * head], both)
        soft_ref[r, 2 * p] = product[:, :seq]
        soft_ref[r, 2 * p + 1] = product[:, seq:]
        return jnp.concatenate(grads, axis=0), inners

    spots = tiles(seq, LANES)

    def finish_row(r):
        wide = [slice(r * seq + t.start, r * seq + t.stop) for t in spots]
        lanes = slice(r * seq, (r + 1) * seq)
        norm_cat[:, lanes] = norm_ref[r]
        gn_ref[:, lanes] = mm(w_ref[...], proj_ref[:, lanes])
        scales = []
        for t in spots:
            n, scale = norm_columns(mc_ref[r, :, t])
            n_ref[r, :, t] = n
            scales.append(scale)
        mean_e = [jnp.zeros((8, LANES), F32) for _ in spots]
        mean_en = [jnp.zeros((8, LANES), F32) for _ in spots]
        for d in tiles(width, 32):
            column = col_ref[3, d]
            gain_sum, shift_sum = acc_ref[3, d], acc_ref[4, d]
            for i, t in enumerate(spots):
                grad_n = gn_ref[d, wide[i]]
                product = grad_n * n_ref[r, d, t]
                gain_sum += product
                shift_sum += grad_n
                mean_e[i] += fold(grad_n * column)
                mean_en[i] += fold(product * column)
            acc_ref[3, d] = gain_sum
            acc_ref[4, d] = shift_sum
        for i, t in enumerate(spots):
            me = jnp.sum(mean_e[i], axis=0, keepdims=True) * (1.0 / width)
            men = jnp.sum(mean_en[i], axis=0, keepdims=True) * (1.0 / width)
            for d in tiles(width, 64):
                e = gn_ref[d, wide[i]] * col_ref[3, d]
                g_ref[r, d, t] = gm_ref[r, d, t] + scales[i] * (e - me - n_ref[r, d, t] * men)
        links, next_links = aux_ref[r, 0:1], aux_ref[r, 1:2]
        for d in tiles(width, 32):
            g = g_ref[r, d]
            base = x_ref[r, d].astype(F32)
            before = pltpu.roll(g, 1, 1) * links
            after = pltpu.roll(g, seq - 1, 1) * next_links
            acc_ref[0, d] += fold_lanes(base * after)
            acc_ref[1, d] += fold_lanes(base * g)
            acc_ref[2, d] += fold_lanes(base * before)
            conv0, conv1, conv2 = [twice(col_ref[i, d], seq) for i in range(3)]
            turn_ref[r, d] = (conv1 * g + conv0 * after + conv2 * before).astype(BF)
        ig_ref[r] = turn_ref[r].T

    ready = opening(*work[0])
    for at, (r, p) in enumerate(work):
        grad_att, inners = ready
        if at + 1 < len(work):
            ready = opening(*work[at + 1])
        for i, h in enumerate((2 * p, 2 * p + 1)):
            for t in tiles(seq, 32):
                raised = e_ref[r, h, t].astype(F32)
                logit_ref[r, h, t] = (raised * (soft_ref[r, h, t] - inners[i])).astype(BF)
        place = slice(r * seq, (r + 1) * seq)
        for i, h in enumerate((2 * p, 2 * p + 1)):
            part = slice(h * head, (h + 1) * head)
            grad_q = mm(k_ref[r, part], logit_ref[r, h]) * head ** (-0.5)
            grad_k = mm_nt(q_ref[r, part], logit_ref[r, h]) * math.log(2.0)
            grad_v = mm_nt(grad_att[i * head : (i + 1) * head], e_ref[r, h])
            for j, grad in enumerate((grad_q, grad_k, grad_v)):
                proj_ref[j * width + h * head : j * width + (h + 1) * head, place] = grad.astype(BF)
        if p == HEADS // 2 - 1:
            finish_row(r)
    w_acc[...] += mm_nt(norm_cat[...], proj_ref[...])

    @pl.when(step == pl.num_programs(0) - 1)
    def _():
        gs_ref[...] = other_ref[...]
        for i in range(5):
            gs_ref[i : i + 1] += jnp.sum(acc_ref[i].T, axis=0, keepdims=True)
        groups = len(gw_refs)
        for i in range(pieces):
            here = pl.ds(pl.multiple_of(index_ref[i] * own, 16), own)
            gw_refs[i % groups][i // groups] = w_acc[here, :].astype(BF)


def in_hbm(values):
    return pltpu.with_memory_space_constraint(values, pltpu.HBM)


def by_row(shape, rows, first=0):
    tail = tuple(shape[1:])
    return pl.BlockSpec((rows,) + tail, lambda i, *_: (i + first,) + (0,) * len(tail))


def whole(shape):
    place = (0,) * len(shape)
    return pl.BlockSpec(tuple(shape), lambda i, *_: place, pipeline_mode=pl.Buffered(1))


def step_rows(count, most):
    return max(r for r in range(1, most + 1) if count % r == 0)


def call(body, name, scalars, rows, row_args, args, row_outs, outs, scratch, span=None, into=None, near=(), only=None, manual=()):
    first, count = span or (0, row_args[0].shape[0])
    skip = first // rows
    total = row_args[0].shape[0]

    def spec_of(shape):
        return by_row(shape, shape[0] * rows // total, skip)

    in_specs = [spec_of(a.shape) for a in row_args]
    if only:
        tail = row_args[0].shape[2:]
        in_specs[0] = pl.BlockSpec((rows, 1) + tail, lambda i, *_: (i, only) + (0,) * len(tail))
    in_specs += [whole(a.shape) for a in args]
    aliases = {}
    if into is not None:
        in_specs.append(pl.BlockSpec(memory_space=pl.ANY))
        aliases = {len(scalars) + len(in_specs) - 1: 0}
    spec = pltpu.PrefetchScalarGridSpec(
        num_scalar_prefetch=len(scalars),
        grid=(count // rows,),
        in_specs=in_specs,
        out_specs=[pl.BlockSpec(memory_space=pl.ANY) for _ in manual] + [spec_of(s) for s, _ in row_outs] + [whole(s) for s, _ in outs],
        scratch_shapes=[pltpu.VMEM(*s) if isinstance(s, tuple) else s for s in scratch],
    )
    return pl.pallas_call(
        body,
        grid_spec=spec,
        out_shape=[pltpu.HBM(s, t) for s, t in manual] + [(jax.ShapeDtypeStruct if "out" + str(i) in near else pltpu.HBM)(s, t) for i, (s, t) in enumerate(row_outs)]
        + [jax.ShapeDtypeStruct(s, t) for s, t in outs],
        input_output_aliases=aliases,
        compiler_params=pltpu.CompilerParams(dimension_semantics=("arbitrary",), vmem_limit_bytes=VMEM_LIMITS[name] * MIB),
        name=name,
    )(*scalars, *[a if i in near else in_hbm(a) for i, a in enumerate(row_args)], *args, *(() if into is None else (into,)))


def small_call(body, name, args, outs, scratch=()):
    return pl.pallas_call(
        body,
        out_shape=[jax.ShapeDtypeStruct(s, t) for s, t in outs],
        scratch_shapes=[pltpu.VMEM(s, t) for s, t in scratch],
        compiler_params=pltpu.CompilerParams(vmem_limit_bytes=16 * MIB),
        name=name,
    )(*args)


def run_forward(index, tokens, segment_ids, valid_len, pieces):
    count, seq, width = tokens.shape
    flipped = (count, width, seq)
    rows = step_rows(count, 3)
    row_outs = [
        ((count, 5, width, seq), BF), (flipped, F32), ((count, seq, width), BF),
        ((count, HEADS, seq, seq), BF), ((count, 16, seq), F32),
    ]
    return call(
        functools.partial(forward_attention, pieces=index.shape[0]), "forward_attention", (index, in_hbm(valid_len)),
        rows, (tokens,), (in_hbm(segment_ids), *pieces),
        row_outs, [((width, VECTORS), BF), ((width, 3 * width), BF)],
        [
            ((3 * width, width), BF), ((width, 3 * width + VECTORS), BF), ((5, width, LANES), F32),
            ((rows, seq, LANES), BF), ((rows, LANES, seq), BF), ((rows, seq, width), BF), ((rows, width, seq), BF),
        ],
    )


def run_feed_forward(index, five, mixed, cotangent, packed, pieces, shards):
    count, seq, width = cotangent.shape
    own = width // index.shape[0]
    ff = shards * width
    groups = 2 if index.shape[0] > 1 else 1
    paired = step_rows(count, 2)
    pairs = 2 if count // paired % 2 == 0 else 1
    rows = pairs * paired
    wide = paired * seq
    manual = [((count // paired, ff, wide), BF), ((count // paired, width, wide), F32)]
    row_outs = [((count, width, seq), F32), ((count, width, seq), BF)]
    grads = ((index.shape[0] // groups, own, 2 * ff + width), BF)
    return call(
        functools.partial(feed_forward, pieces=index.shape[0], shards=shards), "feed_forward", (index,),
        rows, (five, mixed, cotangent), (packed, *pieces),
        row_outs, [((8, width), F32), ((width, ff), BF)] + [grads] * groups,
        [((width, ff), BF)] + [((ff, width), BF)] * 2 + [((width, width), BF)] * 2
        + [((width, ff), F32)] * 2 + [((width, width), F32), ((2, width, LANES), F32), ((3, width, LANES), F32)]
        + [((pairs, width, wide), F32), ((pairs, width, wide), BF), ((pairs, width, wide), BF)]
        + [((pairs, ff, wide), BF)]
        + [((pairs, width, wide), F32), ((pairs, 8, wide), F32), ((pairs, width, wide), BF)]
        + [((pairs, ff, wide), BF), ((pairs, width, wide), F32), pltpu.SemaphoreType.DMA((2, pairs))],
        near=("out1",), only=4, manual=manual,
    )


def run_layer_output(hidden, mixed, down, shape, into, low, high):
    steps = hidden.shape[0]
    span = (int(low * steps), int(high * steps) - int(low * steps))

    def body(*refs):
        layer_output(*refs[:3], refs[-1])

    return call(body, "layer_output", (), 1, (hidden, mixed), (down,), [(shape, BF)], [], [], span=span, into=into)[0]


def run_backward(index, weight, kept, grads, packed, other, pieces):
    count, seq, width = kept[2].shape
    own = width // pieces
    groups = 2 if pieces > 1 else 1
    rows = step_rows(count, 3)
    row_args = (*kept, *grads)
    many = len(row_args)

    def body(index_ref, *refs):
        backward(*refs[:many], index_ref, *refs[many:], pieces=pieces)

    return call(
        body, "backward", (index,), rows, row_args, (weight, packed, other),
        [((count, seq, width), BF)], [((8, width), F32)] + [((pieces // groups, own, 3 * width), BF)] * groups,
        [
            ((3 * width, rows * seq), BF), ((width, 3 * width), F32), ((width, rows * seq), BF),
            ((rows, HEADS, seq, seq), F32), ((rows, HEADS, seq, seq), BF), ((width, rows * seq), F32),
            ((5, width, LANES), F32), ((4, width, LANES), F32), ((rows, width, seq), F32), ((rows, width, seq), F32),
            ((rows, width, seq), BF),
        ],
        near=(5,),
    )


def exchange(values, axis, offset):
    size = lax.axis_size(axis)
    return lax.ppermute(values, axis, [(i, i ^ offset) for i in range(size)])


def add_halves(mine, received):
    count, own, cols = mine.shape

    def body(mine_ref, received_ref, *out_refs):
        for i, ref in enumerate(out_refs):
            ref[...] = (mine_ref[i].astype(F32) + received_ref[i].astype(F32)).astype(BF)

    return small_call(body, "add_halves", (mine, received), [((own, cols), BF)] * count)


def add_wide(*items):
    return tree_sum(item.astype(F32) for item in items)


def store_high_low(ref, cols, values):
    high = values.astype(BF)
    low = (values - high.astype(F32)).astype(BF)
    ref[:, cols:] = jnp.concatenate([high, low, jnp.zeros((ref.shape[0] - 16, LANES), BF)], axis=0)


def load_high_low(ref, cols):
    both = ref[:16, cols:].astype(F32)
    return both[:8] + both[8:]


def add_halves_and_sums(index, mine, received, sums, received_sums):
    count, own, cols = mine.shape
    width = sums.shape[1]

    def body(index_ref, mine_ref, received_ref, sums_ref, received_sums_ref, *out_refs):
        total = sums_ref[...] + received_sums_ref[...]
        for i, ref in enumerate(out_refs):
            ref[:, :cols] = (mine_ref[i].astype(F32) + received_ref[i].astype(F32)).astype(BF)
            turned = pltpu.roll(total, lax.rem(width - index_ref[2 * i] * own, width), 1)[:, :LANES]
            store_high_low(ref, cols, turned)

    spec = pltpu.PrefetchScalarGridSpec(
        num_scalar_prefetch=1, grid=(1,),
        in_specs=[whole(a.shape) for a in (mine, received, sums, received_sums)],
        out_specs=[whole((own, cols + LANES))] * count,
    )
    return pl.pallas_call(
        body, grid_spec=spec, out_shape=[jax.ShapeDtypeStruct((own, cols + LANES), BF)] * count,
        compiler_params=pltpu.CompilerParams(vmem_limit_bytes=16 * MIB), name="add_halves_and_sums",
    )(index, mine, received, sums, received_sums)


def add_packed(name, items):
    cols = items[0].shape[1] - LANES

    def body(*refs):
        out_ref = refs[-1]
        out_ref[:, :cols] = tree_sum(ref[:, :cols].astype(F32) for ref in refs[:-1]).astype(BF)
        store_high_low(out_ref, cols, tree_sum(load_high_low(ref, cols) for ref in refs[:-1]))

    return small_call(body, name, items, [(items[0].shape, BF)])[0]


def add_last(items):
    own, cols = items[0].shape[0], items[0].shape[1] - LANES

    def body(*refs):
        ins, outs = refs[: len(items)], refs[len(items) :]
        outs[0][...] = tree_sum(ref[:, :cols].astype(F32) for ref in ins)
        vectors = tree_sum(load_high_low(ref, cols) for ref in ins)
        outs[1][...] = vectors[0:3, :own]
        for i in range(4):
            outs[2 + i][...] = vectors[3 + i : 4 + i, :own]

    return small_call(body, "add_last", items, [((own, cols), F32), ((3, own), F32)] + [((1, own), F32)] * 4)


def direct_plan(tokens, segment_ids, valid_len, qkv_weight, out_weight, up_weight, down_weight, conv_weight, vectors, cotangent):
    count, seq, width = tokens.shape
    own, ffs = up_weight.shape
    dp, mp = lax.axis_size("dp"), lax.axis_size("mp")
    me = lax.axis_index("dp")
    offsets = [2 * p for p in range(dp // 2)]
    index = jnp.stack([me ^ (p ^ c) for p in offsets for c in range(2)]).astype(jnp.int32)
    narrow, ff_own = small_call(
        pack_weights, "pack_weights",
        [in_hbm(a) for a in (qkv_weight, up_weight, down_weight, conv_weight, *[v.reshape(1, own) for v in vectors])],
        [((own, 3 * width + VECTORS), BF), ((2 * own, ffs), BF)], [((VECTORS, VECTORS), F32)],
    )
    shards = [ff_own] + [exchange(ff_own, "mp", j) for j in range(1, mp)]
    plane = jnp.concatenate([narrow] + [exchange(narrow, "dp", p) for p in offsets[1:]], axis=0)
    pieces = [plane, exchange(plane, "dp", 1)]
    column = jnp.concatenate(shards + [out_weight], axis=0)
    columns = [column] + [exchange(column, "dp", p) for p in offsets[1:]]
    five, mixed, v, raised, facts, packed, weight = run_forward(
        index, tokens, segment_ids, valid_len, pieces
    )
    columns, five = lax.optimization_barrier((columns, five))
    columns = jnp.concatenate(columns, axis=0)
    pieces = [columns, exchange(columns, "dp", 1)]
    hidden, mixed_attn, grad_mixed, grad_att, sums2, down, mine, theirs = run_feed_forward(
        index, five, mixed, cotangent, packed, pieces, mp
    )
    received = exchange(theirs, "dp", 1)
    shape = cotangent.shape
    layer_out = run_layer_output(hidden, mixed_attn, down, shape, None, 0, 0.17)
    received, layer_out = lax.optimization_barrier((received, layer_out))
    parts = list(add_halves(mine, received))
    parts[0], grad_att = lax.optimization_barrier((parts[0], grad_att))
    plane = [parts[0]] + [exchange(parts[i], "dp", p) for i, p in enumerate(offsets) if i]
    kept = (five, mixed, v, raised, facts)
    input_grad, sums, mine_a, theirs_a = run_backward(
        index, weight, kept, (grad_att, grad_mixed), packed, sums2, dp
    )
    plane, theirs_a, sums = lax.optimization_barrier((plane, theirs_a, sums))
    received_a = exchange(theirs_a, "dp", 1)
    received_s = exchange(sums, "dp", 1)
    total = add_wide(*plane).astype(BF)
    total, received_s = lax.optimization_barrier((total, received_s))
    part = 2 * ffs
    near = jnp.concatenate([total[:, :part], total[:, 2 * part : 3 * part]], axis=1)
    out_part = total[:, 4 * part :]
    far = jnp.concatenate([total[:, part : 2 * part], total[:, 3 * part :]], axis=1)
    parts = list(add_halves_and_sums(index, mine_a, received_a, sums, received_s))
    parts[0], hidden, layer_out = lax.optimization_barrier((parts[0], hidden, layer_out))
    plane_a = [parts[0]] + [exchange(parts[i], "dp", p) for i, p in enumerate(offsets) if i]
    received_f = exchange(far, "mp", 1)
    layer_out = run_layer_output(hidden, mixed_attn, down, shape, layer_out, 0.17, 0.51)
    plane_a, layer_out = lax.optimization_barrier((plane_a, layer_out))
    total = add_packed("add_plane", plane_a)
    received_1 = exchange(total, "mp", 1)
    received_f, _ = lax.optimization_barrier((received_f, total))
    near_sum = add_wide(near, received_f[:, : 2 * part])
    out_sum = lax.optimization_barrier(add_wide(out_part, received_f[:, 2 * part :]).astype(BF))
    keep = near_sum[:, :part]
    send = jnp.concatenate([near_sum[:, part:].astype(BF), out_sum], axis=1)
    received_n = exchange(send, "mp", 2)
    layer_out, _ = lax.optimization_barrier((layer_out, send))
    layer_out = run_layer_output(hidden, mixed_attn, down, shape, layer_out, 0.51, 0.67)
    received_1, layer_out = lax.optimization_barrier((received_1, layer_out))
    total = add_packed("add_near", (total, received_1))
    received_2 = exchange(total, "mp", 2)
    layer_out, _ = lax.optimization_barrier((layer_out, total))
    layer_out = run_layer_output(hidden, mixed_attn, down, shape, layer_out, 0.67, 1)
    received_n, layer_out = lax.optimization_barrier((received_n, layer_out))
    grad_up = keep[:, :ffs] + received_n[:, :ffs].astype(F32)
    grad_down = keep[:, ffs:] + received_n[:, ffs : 2 * ffs].astype(F32)
    grad_out = add_wide(out_sum, received_n[:, 2 * ffs :])
    grad_qkv, grad_conv, *grads = add_last((total, received_2))
    return (layer_out, input_grad, grad_qkv, grad_out, grad_up, grad_down, grad_conv, *[g.reshape(own) for g in grads])


def gathered_plan(tokens, segment_ids, valid_len, qkv_weight, out_weight, up_weight, down_weight, conv_weight, vectors, cotangent):
    count, seq, width = tokens.shape
    own = qkv_weight.shape[0]
    dp = width // own
    columns = jnp.stack([conv_weight[0], conv_weight[1], conv_weight[2], *vectors], axis=1)
    narrow = jnp.concatenate([qkv_weight, jnp.pad(columns, ((0, 0), (0, VECTORS - 7))), out_weight], axis=1)
    wide = lax.all_gather(narrow, "dp", axis=0, tiled=True)
    both = lax.all_gather(jnp.concatenate([up_weight, down_weight], axis=0), "mp", axis=1, tiled=True)
    ff = both.shape[1]
    shards = ff // width
    both = lax.all_gather(both, "dp", axis=0).reshape(dp, 2, own, shards, width)
    both = both.transpose(3, 1, 0, 2, 4).reshape(2 * ff, width)
    column = jnp.concatenate([both, wide[:, 3 * width + VECTORS :]], axis=0)
    index = jnp.zeros((1,), jnp.int32)
    five, mixed, v, raised, facts, packed, weight = run_forward(
        index, tokens, segment_ids, valid_len, [wide[:, : 3 * width + VECTORS]]
    )
    hidden, mixed_attn, grad_mixed, grad_att, sums2, down, grads = run_feed_forward(
        index, five, mixed, cotangent, packed, [column], shards
    )
    kept = (five, mixed, v, raised, facts)
    layer_out = run_layer_output(hidden, mixed_attn, down, cotangent.shape, None, 0, 1)
    input_grad, sums, grad_qkv = run_backward(index, weight, kept, (grad_att, grad_mixed), packed, sums2, 1)
    grad_ff = grads[0, :, : 2 * ff].reshape(width, shards, 2, width).transpose(0, 2, 1, 3).reshape(width, 2 * ff)
    grad_ff = lax.psum_scatter(grad_ff, "dp", scatter_dimension=0, tiled=True).reshape(own, 2, ff)
    grad_ff = lax.psum_scatter(grad_ff, "mp", scatter_dimension=2, tiled=True).astype(F32)
    grad_attn = jnp.concatenate([grad_qkv[0], grads[0, :, 2 * ff :]], axis=1)
    grad_attn = lax.psum_scatter(grad_attn, "dp", scatter_dimension=0, tiled=True)
    grad_attn = lax.psum(grad_attn, "mp").astype(F32)
    sums = lax.psum(sums, ("dp", "mp"))
    sums = lax.dynamic_slice_in_dim(sums, lax.axis_index("dp") * own, own, axis=1)
    return (
        layer_out, input_grad, grad_attn[:, : 3 * width], grad_attn[:, 3 * width :],
        grad_ff[:, 0], grad_ff[:, 1], sums[0:3], sums[3], sums[4], sums[5], sums[6],
    )


def on_device(
    tokens, segment_ids, valid_len, qkv_weight, out_weight, up_weight, down_weight, conv_weight,
    ln1_gain, ln1_shift, ln2_gain, ln2_shift, cotangent,
):
    own, ffs = up_weight.shape
    direct = own % 16 == 0 and ffs == tokens.shape[2] and own <= VECTORS and lax.axis_size("mp") == 4
    plan = direct_plan if direct else gathered_plan
    return plan(
        tokens, segment_ids, valid_len, qkv_weight, out_weight, up_weight, down_weight, conv_weight,
        (ln1_gain, ln1_shift, ln2_gain, ln2_shift), cotangent,
    )


def solution(mesh):
    rows = P(("dp", "mp"), None, None)
    weights = (P("dp", None), P("dp", None), P("dp", "mp"), P("dp", "mp"), P(None, "dp"))
    vectors = (P("dp"),) * 4
    return jax.shard_map(
        on_device,
        mesh=mesh,
        in_specs=(rows, P(("dp", "mp"), None), P(("dp", "mp"))) + weights + vectors + (rows,),
        out_specs=(rows, rows) + weights + vectors,
        check_vma=False,
    )
```

profile of v0, /device:TPU:0, one launch (start us, length us, event | category | flops | bytes accessed | tf_op | source)
XLA Modules:
  0.0 136.3 jit_solution(17237006869269462964)
XLA Ops:
  0.7 1.1 pack_weights.1
  1.7 5.1 %collective-permute-start.2 = (bf16[96,384]{1,0:T(8,128)(2,1)S(1)}, bf16[96,384]{1,0:T(8,128)(2,1)S(1)}, u32[]{:S(2)}, u32[]{:S(2)}) collective-permute-start(bf16[96,384]{1,0:T(8,128)(2,1)S(1)} %get-tuple-element.78), channel_id=1, source_target_pairs={{0,3},{1,2},{2,1},{3,0},{4,7},{5,6},{6,5},{7,4},{8,11},{9,10},{10,... | collective-permute-start | bytes 221192 | tf_op jit(solution)/shard_map/ppermute | solution.py:633
  6.8 0.6 collective-permute-start
  7.5 2.6 %collective-permute-start.8 = (bf16[48,1280]{1,0:T(8,128)(2,1)S(1)}, bf16[48,1280]{1,0:T(8,128)(2,1)S(1)}, u32[]{:S(2)}, u32[]{:S(2)}) collective-permute-start(bf16[48,1280]{1,0:T(8,128)(2,1)S(1)} %get-tuple-element.79), channel_id=1, source_target_pairs={{0,24},{4,28},{8,16},{12,20},{16,8},{20,12},{24,0},{28,4},{1,25},{... | collective-permute-start | bytes 368648 | tf_op jit(solution)/shard_map/ppermute | solution.py:633
  10.1 0.5 collective-permute-start.7
  10.6 1.0 collective-permute-done
  11.6 1.5 %collective-permute-start.6 = (bf16[48,1280]{1,0:T(8,128)(2,1)S(1)}, bf16[48,1280]{1,0:T(8,128)(2,1)S(1)}, u32[]{:S(2)}, u32[]{:S(2)}) collective-permute-start(bf16[48,1280]{1,0:T(8,128)(2,1)S(1)} %get-tuple-element.79), channel_id=1, source_target_pairs={{0,8},{4,12},{8,0},{12,4},{16,24},{20,28},{24,16},{28,20},{1,9},{5... | collective-permute-start | bytes 368648 | tf_op jit(solution)/shard_map/ppermute | solution.py:633
  13.1 3.3 %collective-permute-done.6 = bf16[48,1280]{1,0:T(8,128)(2,1)S(1)} collective-permute-done((bf16[48,1280]{1,0:T(8,128)(2,1)S(1)}, bf16[48,1280]{1,0:T(8,128)(2,1)S(1)}, u32[]{:S(2)}, u32[]{:S(2)}) %collective-permute-start.6) | collective-permute-done | bytes 122912 | tf_op jit(solution)/shard_map/ppermute | solution.py:633
  16.7 2.5 %collective-permute-start.5 = (bf16[432,384]{1,0:T(8,128)(2,1)S(1)}, bf16[432,384]{1,0:T(8,128)(2,1)S(1)}, u32[]{:S(2)}, u32[]{:S(2)}) collective-permute-start(bf16[432,384]{1,0:T(8,128)(2,1)S(1)} %constant_dynamic-update-slice_fusion), channel_id=1, source_target_pairs={{0,24},{4,28},{8,16},{12,20},{16,8},{20,12},{24,0},{28,4},{1,25},{... | collective-permute-start | bytes 995336 | tf_op jit(solution)/shard_map/ppermute | solution.py:633
  19.7 0.5 collective-permute-start.3
  20.3 18.2 %forward_attention.1 = (bf16[12,5,384,256]{3,2,1,0:T(8,128)(2,1)}, f32[12,384,256]{2,1,0:T(8,128)}, bf16[12,256,384]{2,1,0:T(8,128)(2,1)}, bf16[12,6,256,256]{3,...) custom-call(s32[8]{0:T(128)S(1)} %stack.35.index_ref, ...), custom_call_target="tpu_custom_call" | custom-call | tf_op jit(solution)/shard_map/forward_attention/pallas_call | solution.py:531
  38.8 3.0 %collective-permute-done.10.refs_1_ = bf16[1728,384]{1,0:T(8,128)(2,1)S(1)} collective-permute-done((bf16[1728,384]{1,0:T(8,128)(2,1)S(1)}, bf16[1728,384]{1,0:T(8,128)(2,1)S(1)}, u32[]{:S(2)}, u32[]{:S(2)}) %collective-permute-start.10) | collective-permute-done | bytes 1327136 | tf_op jit(solution)/shard_map/ppermute | solution.py:633
  41.9 35.5 %feed_forward.1 = (bf16[6,1536,512]{2,1,0:T(8,128)(2,1)}, f32[6,384,512]{2,1,0:T(8,128)}, f32[12,384,256]{2,1,0:T(8,128)}, bf16[12,384,256]{2,1,0:T(8,128)(2,1)S...) custom-call(s32[8]{0:T(128)S(1)} %stack.35.index_ref, ...), custom_call_target="tpu_custom_call" | custom-call | tf_op jit(solution)/shard_map/feed_forward/pallas_call | solution.py:531
  77.6 3.2 %layer_output.4.refs_3_ = bf16[12,256,384]{2,1,0:T(8,128)(2,1)} custom-call(bf16[6,1536,512]{2,1,0:T(8,128)(2,1)} %get-tuple-element.124.refs_0_, f32[6,384,512]{2,1,0:T(8,128)} %get-tuple-element.91.refs_1_, bf16[384,1536]{1,0:T(8,128)(2,1)S(1)} %get-tuple-element.92.refs_2_), custom_call_target="tpu_custom_call" | custom-call | tf_op jit(solution)/shard_map/layer_output/pallas_call | solution.py:531
  81.2 1.6 %collective-permute-start.12 = (bf16[48,3456]{1,0:T(8,128)(2,1)S(1)}, bf16[48,3456]{1,0:T(8,128)(2,1)S(1)}, u32[]{:S(2)}, u32[]{:S(2)}) collective-permute-start(bf16[48,3456]{1,0:T(8,128)(2,1)S(1)} %get-tuple-element.97), channel_id=1, source_target_pairs={{0,8},{4,12},{8,0},{12,4},{16,24},{20,28},{24,16},{28,20},{1,9},{5... | collective-permute-start | bytes 995336 | tf_op jit(solution)/shard_map/ppermute | solution.py:633
  82.7 1.5 %collective-permute-start.13 = (bf16[48,3456]{1,0:T(8,128)(2,1)S(1)}, bf16[48,3456]{1,0:T(8,128)(2,1)S(1)}, u32[]{:S(2)}, u32[]{:S(2)}) collective-permute-start(bf16[48,3456]{1,0:T(8,128)(2,1)S(1)} %get-tuple-element.98), channel_id=1, source_target_pairs={{0,16},{4,20},{8,24},{12,28},{16,0},{20,4},{24,8},{28,12},{1,17},{... | collective-permute-start | bytes 995336 | tf_op jit(solution)/shard_map/ppermute | solution.py:633
  84.7 23.6 %backward.1 = (bf16[12,256,384]{2,1,0:T(8,128)(2,1)}, f32[8,384]{1,0:T(8,128)S(1)}, bf16[4,48,1152]{2,1,0:T(8,128)(2,1)S(1)}, bf16[4,48,1152]{2,1,0:T(8,128)(2,1)S(1)}) custom-call(s32[8]{0:T(128)S(1)} %stack.35.index_ref, bf16[12,5,384,256]{3,2,1,0:T(8,128)(2,1)} %get-tuple-element.81.five_ref.refs_0_, f32[12,384,256]{2,1,0:T(8,128)} %get-tuple-element.82.mc_ref.refs_1_, ...), custom_call_target="tpu_custom_call" | custom-call | tf_op jit(solution)/shard_map/backward/pallas_call | solution.py:531
  109.7 2.5 %collective-permute-start.16 = (bf16[48,1920]{1,0:T(8,128)(2,1)S(1)}, bf16[48,1920]{1,0:T(8,128)(2,1)S(1)}, u32[]{:S(2)}, u32[]{:S(2)}) collective-permute-start(bf16[48,1920]{1,0:T(8,128)(2,1)S(1)} %pad_maximum_fusion), channel_id=1, source_target_pairs={{0,1},{1,0},{2,3},{3,2},{4,5},{5,4},{6,7},{7,6},{8,9},{9,8},{10,11... | collective-permute-start | bytes 552968 | tf_op jit(solution)/shard_map/ppermute | solution.py:633
  112.2 0.7 add_halves_and_sums.1
  113.0 1.6 %collective-permute-start.18 = (bf16[48,1280]{1,0:T(8,128)(2,1)S(1)}, bf16[48,1280]{1,0:T(8,128)(2,1)S(1)}, u32[]{:S(2)}, u32[]{:S(2)}) collective-permute-start(bf16[48,1280]{1,0:T(8,128)(2,1)S(1)} %get-tuple-element.121), channel_id=1, source_target_pairs={{0,8},{4,12},{8,0},{12,4},{16,24},{20,28},{24,16},{28,20},{1,9},{5... | collective-permute-start | bytes 368648 | tf_op jit(solution)/shard_map/ppermute | solution.py:633
  114.5 1.5 %collective-permute-start.19 = (bf16[48,1280]{1,0:T(8,128)(2,1)S(1)}, bf16[48,1280]{1,0:T(8,128)(2,1)S(1)}, u32[]{:S(2)}, u32[]{:S(2)}) collective-permute-start(bf16[48,1280]{1,0:T(8,128)(2,1)S(1)} %get-tuple-element.122), channel_id=1, source_target_pairs={{0,16},{4,20},{8,24},{12,28},{16,0},{20,4},{24,8},{28,12},{1,17},{... | collective-permute-start | bytes 368648 | tf_op jit(solution)/shard_map/ppermute | solution.py:633
  116.5 4.1 %layer_output.5.refs_3_ = bf16[12,256,384]{2,1,0:T(8,128)(2,1)} custom-call(bf16[6,1536,512]{2,1,0:T(8,128)(2,1)} %get-tuple-element.124.refs_0_, f32[6,384,512]{2,1,0:T(8,128)} %get-tuple-element.91.refs_1_, bf16[384,1536]{1,0:T(8,128)(2,1)S(1)} %get-tuple-element.92.refs_2_, bf16[12,256,384]{2,1,0:T(8,128)(2,1)} %layer_output.4.refs_3_), custom_call_target="tpu_custom_call", output_to_operand_aliasing={{}: (3, {})} | custom-call | tf_op jit(solution)/shard_map/layer_output/pallas_call | solution.py:531
  120.6 1.4 %collective-permute-done.19.refs_2_ = bf16[48,1280]{1,0:T(8,128)(2,1)S(1)} collective-permute-done((bf16[48,1280]{1,0:T(8,128)(2,1)S(1)}, bf16[48,1280]{1,0:T(8,128)(2,1)S(1)}, u32[]{:S(2)}, u32[]{:S(2)}) %collective-permute-start.19) | collective-permute-done | bytes 122912 | tf_op jit(solution)/shard_map/ppermute | solution.py:633
  122.1 1.1 collective-permute-start.22
  123.3 1.4 %collective-permute-start.21 = (bf16[48,1152]{1,0:T(8,128)(2,1)S(1)}, bf16[48,1152]{1,0:T(8,128)(2,1)S(1)}, u32[]{:S(2)}, u32[]{:S(2)}) collective-permute-start(bf16[48,1152]{1,0:T(8,128)(2,1)S(1)} %pad_maximum_fusion.1), channel_id=1, source_target_pairs={{0,2},{1,3},{2,0},{3,1},{4,6},{5,7},{6,4},{7,5},{8,10},{9,11},{10,... | collective-permute-start | bytes 331784 | tf_op jit(solution)/shard_map/ppermute | solution.py:633
  124.7 3.2 %layer_output.6.refs_3_ = bf16[12,256,384]{2,1,0:T(8,128)(2,1)} custom-call(bf16[6,1536,512]{2,1,0:T(8,128)(2,1)} %get-tuple-element.124.refs_0_, f32[6,384,512]{2,1,0:T(8,128)} %get-tuple-element.91.refs_1_, bf16[384,1536]{1,0:T(8,128)(2,1)S(1)} %get-tuple-element.92.refs_2_, bf16[12,256,384]{2,1,0:T(8,128)(2,1)} %layer_output.5.refs_3_), custom_call_target="tpu_custom_call", output_to_operand_aliasing={{}: (3, {})} | custom-call | tf_op jit(solution)/shard_map/layer_output/pallas_call | solution.py:531
  127.9 0.8 collective-permute-done.22.refs_1_
  128.8 0.9 collective-permute-start.23
  129.6 4.1 %layer_output.7 = bf16[12,256,384]{2,1,0:T(8,128)(2,1)} custom-call(bf16[6,1536,512]{2,1,0:T(8,128)(2,1)} %get-tuple-element.124.refs_0_, f32[6,384,512]{2,1,0:T(8,128)} %get-tuple-element.91.refs_1_, bf16[384,1536]{1,0:T(8,128)(2,1)S(1)} %get-tuple-element.92.refs_2_, bf16[12,256,384]{2,1,0:T(8,128)(2,1)} %layer_output.6.refs_3_), custom_call_target="tpu_custom_call", output_to_operand_aliasing={{}: (3, {})} | custom-call | tf_op jit(solution)/shard_map/layer_output/pallas_call | solution.py:531
  133.7 0.7 slice_add_fusion
  134.4 1.1 collective-permute-done.23.refs_1_
  135.5 0.7 add_last.1
  (54 shorter events, 4.0 us)
Async XLA Ops:
  0.6 16.0 %copy-start = (bf16[48,384]{1,0:T(8,128)(2,1)S(1)}, bf16[48,384]{1,0:T(8,128)(2,1)}, u32[]{:S(2)}) copy-start(bf16[48,384]{1,0:T(8,128)(2,1)} %param.17) | copy-start | bytes 110596
  1.7 14.9 %collective-permute-start.2 = (bf16[96,384]{1,0:T(8,128)(2,1)S(1)}, bf16[96,384]{1,0:T(8,128)(2,1)S(1)}, u32[]{:S(2)}, u32[]{:S(2)}) collective-permute-start(bf16[96,384]{1,0:T(8,128)(2,1)S(1)} %get-tuple-element.78), channel_id=1, source_target_pairs={{0,3},{1,2},{2,1},{3,0},{4,7},{5,6},{6,5},{7,4},{8,11},{9,10},{10,... | collective-permute-start | bytes 221192 | tf_op jit(solution)/shard_map/ppermute | solution.py:633
  6.8 6.2 %collective-permute-start.1 = (bf16[96,384]{1,0:T(8,128)(2,1)S(1)}, bf16[96,384]{1,0:T(8,128)(2,1)S(1)}, u32[]{:S(2)}, u32[]{:S(2)}) collective-permute-start(bf16[96,384]{1,0:T(8,128)(2,1)S(1)} %get-tuple-element.78), channel_id=1, source_target_pairs={{0,2},{1,3},{2,0},{3,1},{4,6},{5,7},{6,4},{7,5},{8,10},{9,11},{10,... | collective-permute-start | bytes 221192 | tf_op jit(solution)/shard_map/ppermute | solution.py:633
  6.8 4.7 %collective-permute-start = (bf16[96,384]{1,0:T(8,128)(2,1)S(1)}, bf16[96,384]{1,0:T(8,128)(2,1)S(1)}, u32[]{:S(2)}, u32[]{:S(2)}) collective-permute-start(bf16[96,384]{1,0:T(8,128)(2,1)S(1)} %get-tuple-element.78), channel_id=1, source_target_pairs={{0,1},{1,0},{2,3},{3,2},{4,5},{5,4},{6,7},{7,6},{8,9},{9,8},{10,11... | collective-permute-start | bytes 221192 | tf_op jit(solution)/shard_map/ppermute | solution.py:633
  7.5 9.0 %collective-permute-start.8 = (bf16[48,1280]{1,0:T(8,128)(2,1)S(1)}, bf16[48,1280]{1,0:T(8,128)(2,1)S(1)}, u32[]{:S(2)}, u32[]{:S(2)}) collective-permute-start(bf16[48,1280]{1,0:T(8,128)(2,1)S(1)} %get-tuple-element.79), channel_id=1, source_target_pairs={{0,24},{4,28},{8,16},{12,20},{16,8},{20,12},{24,0},{28,4},{1,25},{... | collective-permute-start | bytes 368648 | tf_op jit(solution)/shard_map/ppermute | solution.py:633
  10.1 6.4 %collective-permute-start.7 = (bf16[48,1280]{1,0:T(8,128)(2,1)S(1)}, bf16[48,1280]{1,0:T(8,128)(2,1)S(1)}, u32[]{:S(2)}, u32[]{:S(2)}) collective-permute-start(bf16[48,1280]{1,0:T(8,128)(2,1)S(1)} %get-tuple-element.79), channel_id=1, source_target_pairs={{0,16},{4,20},{8,24},{12,28},{16,0},{20,4},{24,8},{28,12},{1,17},{... | collective-permute-start | bytes 368648 | tf_op jit(solution)/shard_map/ppermute | solution.py:633
  11.6 4.9 %collective-permute-start.6 = (bf16[48,1280]{1,0:T(8,128)(2,1)S(1)}, bf16[48,1280]{1,0:T(8,128)(2,1)S(1)}, u32[]{:S(2)}, u32[]{:S(2)}) collective-permute-start(bf16[48,1280]{1,0:T(8,128)(2,1)S(1)} %get-tuple-element.79), channel_id=1, source_target_pairs={{0,8},{4,12},{8,0},{12,4},{16,24},{20,28},{24,16},{28,20},{1,9},{5... | collective-permute-start | bytes 368648 | tf_op jit(solution)/shard_map/ppermute | solution.py:633
  16.5 3.8 %collective-permute-start.9 = (bf16[192,1280]{1,0:T(8,128)(2,1)S(1)}, bf16[192,1280]{1,0:T(8,128)(2,1)S(1)}, u32[]{:S(2)}, u32[]{:S(2)}) collective-permute-start(bf16[192,1280]{1,0:T(8,128)(2,1)S(1)} %constant_dynamic-update-slice_fusion.5.refs_0_), channel_id=1, source_target_pairs={{0,4},{4,0},{8,12},{12,8},{16,20},{20,16},{24,28},{28,24},{1,5},{5... | collective-permute-start | bytes 1474568 | tf_op jit(solution)/shard_map/ppermute | solution.py:633
  16.7 21.8 %collective-permute-start.5 = (bf16[432,384]{1,0:T(8,128)(2,1)S(1)}, bf16[432,384]{1,0:T(8,128)(2,1)S(1)}, u32[]{:S(2)}, u32[]{:S(2)}) collective-permute-start(bf16[432,384]{1,0:T(8,128)(2,1)S(1)} %constant_dynamic-update-slice_fusion), channel_id=1, source_target_pairs={{0,24},{4,28},{8,16},{12,20},{16,8},{20,12},{24,0},{28,4},{1,25},{... | collective-permute-start | bytes 995336 | tf_op jit(solution)/shard_map/ppermute | solution.py:633
  19.2 19.3 %collective-permute-start.4 = (bf16[432,384]{1,0:T(8,128)(2,1)S(1)}, bf16[432,384]{1,0:T(8,128)(2,1)S(1)}, u32[]{:S(2)}, u32[]{:S(2)}) collective-permute-start(bf16[432,384]{1,0:T(8,128)(2,1)S(1)} %constant_dynamic-update-slice_fusion), channel_id=1, source_target_pairs={{0,16},{4,20},{8,24},{12,28},{16,0},{20,4},{24,8},{28,12},{1,17},{... | collective-permute-start | bytes 995336 | tf_op jit(solution)/shard_map/ppermute | solution.py:633
  19.7 18.8 %collective-permute-start.3 = (bf16[432,384]{1,0:T(8,128)(2,1)S(1)}, bf16[432,384]{1,0:T(8,128)(2,1)S(1)}, u32[]{:S(2)}, u32[]{:S(2)}) collective-permute-start(bf16[432,384]{1,0:T(8,128)(2,1)S(1)} %constant_dynamic-update-slice_fusion), channel_id=1, source_target_pairs={{0,8},{4,12},{8,0},{12,4},{16,24},{20,28},{24,16},{28,20},{1,9},{5... | collective-permute-start | bytes 995336 | tf_op jit(solution)/shard_map/ppermute | solution.py:633
  38.8 3.1 %collective-permute-start.10 = (bf16[1728,384]{1,0:T(8,128)(2,1)S(1)}, bf16[1728,384]{1,0:T(8,128)(2,1)S(1)}, u32[]{:S(2)}, u32[]{:S(2)}) collective-permute-start(bf16[1728,384]{1,0:T(8,128)(2,1)S(1)} %constant_dynamic-update-slice_fusion.9.refs_0_), channel_id=1, source_target_pairs={{0,4},{4,0},{8,12},{12,8},{16,20},{20,16},{24,28},{28,24},{1,5},{5... | collective-permute-start | bytes 3981320 | tf_op jit(solution)/shard_map/ppermute | solution.py:633
  77.4 3.4 %collective-permute-start.11 = (bf16[4,48,3456]{2,1,0:T(8,128)(2,1)S(1)}, bf16[4,48,3456]{2,1,0:T(8,128)(2,1)S(1)}, u32[]{:S(2)}, u32[]{:S(2)}) collective-permute-start(bf16[4,48,3456]{2,1,0:T(8,128)(2,1)S(1)} %get-tuple-element.89), channel_id=1, source_target_pairs={{0,4},{4,0},{8,12},{12,8},{16,20},{20,16},{24,28},{28,24},{1,5},{5... | collective-permute-start | bytes 3981320 | tf_op jit(solution)/shard_map/ppermute | solution.py:633
  81.2 27.2 %collective-permute-start.12 = (bf16[48,3456]{1,0:T(8,128)(2,1)S(1)}, bf16[48,3456]{1,0:T(8,128)(2,1)S(1)}, u32[]{:S(2)}, u32[]{:S(2)}) collective-permute-start(bf16[48,3456]{1,0:T(8,128)(2,1)S(1)} %get-tuple-element.97), channel_id=1, source_target_pairs={{0,8},{4,12},{8,0},{12,4},{16,24},{20,28},{24,16},{28,20},{1,9},{5... | collective-permute-start | bytes 995336 | tf_op jit(solution)/shard_map/ppermute | solution.py:633
  82.7 25.6 %collective-permute-start.13 = (bf16[48,3456]{1,0:T(8,128)(2,1)S(1)}, bf16[48,3456]{1,0:T(8,128)(2,1)S(1)}, u32[]{:S(2)}, u32[]{:S(2)}) collective-permute-start(bf16[48,3456]{1,0:T(8,128)(2,1)S(1)} %get-tuple-element.98), channel_id=1, source_target_pairs={{0,16},{4,20},{8,24},{12,28},{16,0},{20,4},{24,8},{28,12},{1,17},{... | collective-permute-start | bytes 995336 | tf_op jit(solution)/shard_map/ppermute | solution.py:633
  84.3 24.1 %collective-permute-start.14 = (bf16[48,3456]{1,0:T(8,128)(2,1)S(1)}, bf16[48,3456]{1,0:T(8,128)(2,1)S(1)}, u32[]{:S(2)}, u32[]{:S(2)}) collective-permute-start(bf16[48,3456]{1,0:T(8,128)(2,1)S(1)} %get-tuple-element.99), channel_id=1, source_target_pairs={{0,24},{4,28},{8,16},{12,20},{16,8},{20,12},{24,0},{28,4},{1,25},{... | collective-permute-start | bytes 995336 | tf_op jit(solution)/shard_map/ppermute | solution.py:633
  108.4 1.2 collective-permute-start.15
  108.5 3.8 %collective-permute-start.17 = (bf16[4,48,1152]{2,1,0:T(8,128)(2,1)S(1)}, bf16[4,48,1152]{2,1,0:T(8,128)(2,1)S(1)}, u32[]{:S(2)}, u32[]{:S(2)}) collective-permute-start(bf16[4,48,1152]{2,1,0:T(8,128)(2,1)S(1)} %get-tuple-element.116), channel_id=1, source_target_pairs={{0,4},{4,0},{8,12},{12,8},{16,20},{20,16},{24,28},{28,24},{1,5},{5... | collective-permute-start | bytes 1327112 | tf_op jit(solution)/shard_map/ppermute | solution.py:633
  109.7 13.6 %collective-permute-start.16 = (bf16[48,1920]{1,0:T(8,128)(2,1)S(1)}, bf16[48,1920]{1,0:T(8,128)(2,1)S(1)}, u32[]{:S(2)}, u32[]{:S(2)}) collective-permute-start(bf16[48,1920]{1,0:T(8,128)(2,1)S(1)} %pad_maximum_fusion), channel_id=1, source_target_pairs={{0,1},{1,0},{2,3},{3,2},{4,5},{5,4},{6,7},{7,6},{8,9},{9,8},{10,11... | collective-permute-start | bytes 552968 | tf_op jit(solution)/shard_map/ppermute | solution.py:633
  113.0 7.6 %collective-permute-start.18 = (bf16[48,1280]{1,0:T(8,128)(2,1)S(1)}, bf16[48,1280]{1,0:T(8,128)(2,1)S(1)}, u32[]{:S(2)}, u32[]{:S(2)}) collective-permute-start(bf16[48,1280]{1,0:T(8,128)(2,1)S(1)} %get-tuple-element.121), channel_id=1, source_target_pairs={{0,8},{4,12},{8,0},{12,4},{16,24},{20,28},{24,16},{28,20},{1,9},{5... | collective-permute-start | bytes 368648 | tf_op jit(solution)/shard_map/ppermute | solution.py:633
  114.5 7.5 %collective-permute-start.19 = (bf16[48,1280]{1,0:T(8,128)(2,1)S(1)}, bf16[48,1280]{1,0:T(8,128)(2,1)S(1)}, u32[]{:S(2)}, u32[]{:S(2)}) collective-permute-start(bf16[48,1280]{1,0:T(8,128)(2,1)S(1)} %get-tuple-element.122), channel_id=1, source_target_pairs={{0,16},{4,20},{8,24},{12,28},{16,0},{20,4},{24,8},{28,12},{1,17},{... | collective-permute-start | bytes 368648 | tf_op jit(solution)/shard_map/ppermute | solution.py:633
  116.1 6.0 %collective-permute-start.20 = (bf16[48,1280]{1,0:T(8,128)(2,1)S(1)}, bf16[48,1280]{1,0:T(8,128)(2,1)S(1)}, u32[]{:S(2)}, u32[]{:S(2)}) collective-permute-start(bf16[48,1280]{1,0:T(8,128)(2,1)S(1)} %get-tuple-element.123), channel_id=1, source_target_pairs={{0,24},{4,28},{8,16},{12,20},{16,8},{20,12},{24,0},{28,4},{1,25},{... | collective-permute-start | bytes 368648 | tf_op jit(solution)/shard_map/ppermute | solution.py:633
  122.1 6.6 %collective-permute-start.22 = (bf16[48,1280]{1,0:T(8,128)(2,1)S(1)}, bf16[48,1280]{1,0:T(8,128)(2,1)S(1)}, u32[]{:S(2)}, u32[]{:S(2)}) collective-permute-start(bf16[48,1280]{1,0:T(8,128)(2,1)S(1)} %add_plane.1.refs_0_), channel_id=1, source_target_pairs={{0,1},{1,0},{2,3},{3,2},{4,5},{5,4},{6,7},{7,6},{8,9},{9,8},{10,11... | collective-permute-start | bytes 368648 | tf_op jit(solution)/shard_map/ppermute | solution.py:633
  123.3 10.4 %collective-permute-start.21 = (bf16[48,1152]{1,0:T(8,128)(2,1)S(1)}, bf16[48,1152]{1,0:T(8,128)(2,1)S(1)}, u32[]{:S(2)}, u32[]{:S(2)}) collective-permute-start(bf16[48,1152]{1,0:T(8,128)(2,1)S(1)} %pad_maximum_fusion.1), channel_id=1, source_target_pairs={{0,2},{1,3},{2,0},{3,1},{4,6},{5,7},{6,4},{7,5},{8,10},{9,11},{10,... | collective-permute-start | bytes 331784 | tf_op jit(solution)/shard_map/ppermute | solution.py:633
  128.8 6.8 %collective-permute-start.23 = (bf16[48,1280]{1,0:T(8,128)(2,1)S(1)}, bf16[48,1280]{1,0:T(8,128)(2,1)S(1)}, u32[]{:S(2)}, u32[]{:S(2)}) collective-permute-start(bf16[48,1280]{1,0:T(8,128)(2,1)S(1)} %add_near.1.refs_0_), channel_id=1, source_target_pairs={{0,2},{1,3},{2,0},{3,1},{4,6},{5,7},{6,4},{7,5},{8,10},{9,11},{10,... | collective-permute-start | bytes 368648 | tf_op jit(solution)/shard_map/ppermute | solution.py:633
where the time goes:
time: 137 us; the launch traced here: 136 us
  Pallas kernels  94.8 us (69%)
  starting transfers between devices  27.9 us (20%)
  waiting for transfers between devices  11.2 us (8%)
    pallas_call x7, Pallas kernels, call(): pl.pallas_call(body, grid_spec=spec, out_shape=[pltpu.HBM(s, t) for s, t...  91.9 us
    ppermute x24, starting transfers between devices, exchange(): return lax.ppermute(values, axis, [(i, i ^ offset) for i in range(size)])  27.9 us
    ppermute x24, waiting for transfers between devices, exchange(): return lax.ppermute(values, axis, [(i, i ^ offset) for i in range(size)])  11.2 us
  transfers between devices with their start and end apart: 24, of which 7 were waited for; matrix products, arithmetic and copies ran while one was open for 1% of the time, Pallas kernels for 42%

commit v1 on v0

--- a/solution.py
+++ b/solution.py
@@ -490,6 +490,10 @@
     return pltpu.with_memory_space_constraint(values, pltpu.HBM)
 
 
+def in_vmem(values):
+    return pltpu.with_memory_space_constraint(values, pltpu.VMEM)
+
+
 def by_row(shape, rows, first=0):
     tail = tuple(shape[1:])
     return pl.BlockSpec((rows,) + tail, lambda i, *_: (i + first,) + (0,) * len(tail))
@@ -516,7 +520,7 @@
     if only:
         tail = row_args[0].shape[2:]
         in_specs[0] = pl.BlockSpec((rows, 1) + tail, lambda i, *_: (i, only) + (0,) * len(tail))
-    in_specs += [whole(a.shape) for a in args]
+    in_specs += [whole(a.shape) if a.dtype == jnp.int32 else pl.BlockSpec(memory_space=pltpu.VMEM) for a in args]
     aliases = {}
     if into is not None:
         in_specs.append(pl.BlockSpec(memory_space=pl.ANY))
@@ -536,7 +540,7 @@
         input_output_aliases=aliases,
         compiler_params=pltpu.CompilerParams(dimension_semantics=("arbitrary",), vmem_limit_bytes=VMEM_LIMITS[name] * MIB),
         name=name,
-    )(*scalars, *[a if i in near else in_hbm(a) for i, a in enumerate(row_args)], *args, *(() if into is None else (into,)))
+    )(*scalars, *[a if i in near else in_hbm(a) for i, a in enumerate(row_args)], *[in_hbm(a) if a.dtype == jnp.int32 else in_vmem(a) for a in args], *(() if into is None else (into,)))
 
 
 def small_call(body, name, args, outs, scratch=()):
@@ -559,7 +563,7 @@
     ]
     return call(
         functools.partial(forward_attention, pieces=index.shape[0]), "forward_attention", (index, in_hbm(valid_len)),
-        rows, (tokens,), (in_hbm(segment_ids), *pieces),
+        rows, (tokens,), (segment_ids, *pieces),
         row_outs, [((width, VECTORS), BF), ((width, 3 * width), BF)],
         [
             ((3 * width, width), BF), ((width, 3 * width + VECTORS), BF), ((5, width, LANES), F32),

time: 137 us -> 137 us (level)
  no operation moved by 1% of the time
where the time goes in v1:
time: 137 us; the launch traced here: 136 us
  Pallas kernels  94.8 us (69%)
  starting transfers between devices  27.9 us (20%)
  waiting for transfers between devices  11.2 us (8%)
    pallas_call x7, Pallas kernels, call(): pl.pallas_call(body, grid_spec=spec, out_shape=[pltpu.HBM(s, t) for s, t...  91.9 us
    ppermute x24, starting transfers between devices, exchange(): return lax.ppermute(values, axis, [(i, i ^ offset) for i in range(size)])  27.9 us
    ppermute x24, waiting for transfers between devices, exchange(): return lax.ppermute(values, axis, [(i, i ^ offset) for i in range(size)])  11.2 us
  transfers between devices with their start and end apart: 24, of which 7 were waited for; matrix products, arithmetic and copies ran while one was open for 1% of the time, Pallas kernels for 42%

profile of v1, /device:TPU:0, one launch (start us, length us, event | category | flops | bytes accessed | tf_op | source)
XLA Modules:
  0.0 136.3 jit_solution(17237006869269462964)
XLA Ops:
  0.7 1.1 pack_weights.1
  1.7 5.1 %collective-permute-start.2 = (bf16[96,384]{1,0:T(8,128)(2,1)S(1)}, bf16[96,384]{1,0:T(8,128)(2,1)S(1)}, u32[]{:S(2)}, u32[]{:S(2)}) collective-permute-start(bf16[96,384]{1,0:T(8,128)(2,1)S(1)} %get-tuple-element.78), channel_id=1, source_target_pairs={{0,3},{1,2},{2,1},{3,0},{4,7},{5,6},{6,5},{7,4},{8,11},{9,10},{10,... | collective-permute-start | bytes 221192 | tf_op jit(solution)/shard_map/ppermute | solution.py:637
  6.8 0.6 collective-permute-start
  7.5 2.6 %collective-permute-start.8 = (bf16[48,1280]{1,0:T(8,128)(2,1)S(1)}, bf16[48,1280]{1,0:T(8,128)(2,1)S(1)}, u32[]{:S(2)}, u32[]{:S(2)}) collective-permute-start(bf16[48,1280]{1,0:T(8,128)(2,1)S(1)} %get-tuple-element.79), channel_id=1, source_target_pairs={{0,24},{4,28},{8,16},{12,20},{16,8},{20,12},{24,0},{28,4},{1,25},{... | collective-permute-start | bytes 368648 | tf_op jit(solution)/shard_map/ppermute | solution.py:637
  10.1 0.5 collective-permute-start.7
  10.6 1.0 collective-permute-done
  11.6 1.5 %collective-permute-start.6 = (bf16[48,1280]{1,0:T(8,128)(2,1)S(1)}, bf16[48,1280]{1,0:T(8,128)(2,1)S(1)}, u32[]{:S(2)}, u32[]{:S(2)}) collective-permute-start(bf16[48,1280]{1,0:T(8,128)(2,1)S(1)} %get-tuple-element.79), channel_id=1, source_target_pairs={{0,8},{4,12},{8,0},{12,4},{16,24},{20,28},{24,16},{28,20},{1,9},{5... | collective-permute-start | bytes 368648 | tf_op jit(solution)/shard_map/ppermute | solution.py:637
  13.1 3.3 %collective-permute-done.6 = bf16[48,1280]{1,0:T(8,128)(2,1)S(1)} collective-permute-done((bf16[48,1280]{1,0:T(8,128)(2,1)S(1)}, bf16[48,1280]{1,0:T(8,128)(2,1)S(1)}, u32[]{:S(2)}, u32[]{:S(2)}) %collective-permute-start.6) | collective-permute-done | bytes 122912 | tf_op jit(solution)/shard_map/ppermute | solution.py:637
  16.7 2.5 %collective-permute-start.5 = (bf16[432,384]{1,0:T(8,128)(2,1)S(1)}, bf16[432,384]{1,0:T(8,128)(2,1)S(1)}, u32[]{:S(2)}, u32[]{:S(2)}) collective-permute-start(bf16[432,384]{1,0:T(8,128)(2,1)S(1)} %constant_dynamic-update-slice_fusion), channel_id=1, source_target_pairs={{0,24},{4,28},{8,16},{12,20},{16,8},{20,12},{24,0},{28,4},{1,25},{... | collective-permute-start | bytes 995336 | tf_op jit(solution)/shard_map/ppermute | solution.py:637
  19.7 0.5 collective-permute-start.3
  20.3 18.2 %forward_attention.1 = (bf16[12,5,384,256]{3,2,1,0:T(8,128)(2,1)}, f32[12,384,256]{2,1,0:T(8,128)}, bf16[12,256,384]{2,1,0:T(8,128)(2,1)}, bf16[12,6,256,256]{3,...) custom-call(s32[8]{0:T(128)S(1)} %stack.35.index_ref, ...), custom_call_target="tpu_custom_call" | custom-call | tf_op jit(solution)/shard_map/forward_attention/pallas_call | solution.py:535
  38.8 3.0 %collective-permute-done.10.refs_1_ = bf16[1728,384]{1,0:T(8,128)(2,1)S(1)} collective-permute-done((bf16[1728,384]{1,0:T(8,128)(2,1)S(1)}, bf16[1728,384]{1,0:T(8,128)(2,1)S(1)}, u32[]{:S(2)}, u32[]{:S(2)}) %collective-permute-start.10) | collective-permute-done | bytes 1327136 | tf_op jit(solution)/shard_map/ppermute | solution.py:637
  41.9 35.5 %feed_forward.1 = (bf16[6,1536,512]{2,1,0:T(8,128)(2,1)}, f32[6,384,512]{2,1,0:T(8,128)}, f32[12,384,256]{2,1,0:T(8,128)}, bf16[12,384,256]{2,1,0:T(8,128)(2,1)S...) custom-call(s32[8]{0:T(128)S(1)} %stack.35.index_ref, ...), custom_call_target="tpu_custom_call" | custom-call | tf_op jit(solution)/shard_map/feed_forward/pallas_call | solution.py:535
  77.6 3.2 %layer_output.4.refs_3_ = bf16[12,256,384]{2,1,0:T(8,128)(2,1)} custom-call(bf16[6,1536,512]{2,1,0:T(8,128)(2,1)} %get-tuple-element.124.refs_0_, f32[6,384,512]{2,1,0:T(8,128)} %get-tuple-element.91.refs_1_, bf16[384,1536]{1,0:T(8,128)(2,1)S(1)} %get-tuple-element.92.refs_2_), custom_call_target="tpu_custom_call" | custom-call | tf_op jit(solution)/shard_map/layer_output/pallas_call | solution.py:535
  81.2 1.6 %collective-permute-start.12 = (bf16[48,3456]{1,0:T(8,128)(2,1)S(1)}, bf16[48,3456]{1,0:T(8,128)(2,1)S(1)}, u32[]{:S(2)}, u32[]{:S(2)}) collective-permute-start(bf16[48,3456]{1,0:T(8,128)(2,1)S(1)} %get-tuple-element.97), channel_id=1, source_target_pairs={{0,8},{4,12},{8,0},{12,4},{16,24},{20,28},{24,16},{28,20},{1,9},{5... | collective-permute-start | bytes 995336 | tf_op jit(solution)/shard_map/ppermute | solution.py:637
  82.7 1.5 %collective-permute-start.13 = (bf16[48,3456]{1,0:T(8,128)(2,1)S(1)}, bf16[48,3456]{1,0:T(8,128)(2,1)S(1)}, u32[]{:S(2)}, u32[]{:S(2)}) collective-permute-start(bf16[48,3456]{1,0:T(8,128)(2,1)S(1)} %get-tuple-element.98), channel_id=1, source_target_pairs={{0,16},{4,20},{8,24},{12,28},{16,0},{20,4},{24,8},{28,12},{1,17},{... | collective-permute-start | bytes 995336 | tf_op jit(solution)/shard_map/ppermute | solution.py:637
  84.7 23.6 %backward.1 = (bf16[12,256,384]{2,1,0:T(8,128)(2,1)}, f32[8,384]{1,0:T(8,128)S(1)}, bf16[4,48,1152]{2,1,0:T(8,128)(2,1)S(1)}, bf16[4,48,1152]{2,1,0:T(8,128)(2,1)S(1)}) custom-call(s32[8]{0:T(128)S(1)} %stack.35.index_ref, bf16[12,5,384,256]{3,2,1,0:T(8,128)(2,1)} %get-tuple-element.81.five_ref.refs_0_, f32[12,384,256]{2,1,0:T(8,128)} %get-tuple-element.82.mc_ref.refs_1_, ...), custom_call_target="tpu_custom_call" | custom-call | tf_op jit(solution)/shard_map/backward/pallas_call | solution.py:535
  109.7 2.5 %collective-permute-start.16 = (bf16[48,1920]{1,0:T(8,128)(2,1)S(1)}, bf16[48,1920]{1,0:T(8,128)(2,1)S(1)}, u32[]{:S(2)}, u32[]{:S(2)}) collective-permute-start(bf16[48,1920]{1,0:T(8,128)(2,1)S(1)} %pad_maximum_fusion), channel_id=1, source_target_pairs={{0,1},{1,0},{2,3},{3,2},{4,5},{5,4},{6,7},{7,6},{8,9},{9,8},{10,11... | collective-permute-start | bytes 552968 | tf_op jit(solution)/shard_map/ppermute | solution.py:637
  112.2 0.7 add_halves_and_sums.1
  113.0 1.6 %collective-permute-start.18 = (bf16[48,1280]{1,0:T(8,128)(2,1)S(1)}, bf16[48,1280]{1,0:T(8,128)(2,1)S(1)}, u32[]{:S(2)}, u32[]{:S(2)}) collective-permute-start(bf16[48,1280]{1,0:T(8,128)(2,1)S(1)} %get-tuple-element.121), channel_id=1, source_target_pairs={{0,8},{4,12},{8,0},{12,4},{16,24},{20,28},{24,16},{28,20},{1,9},{5... | collective-permute-start | bytes 368648 | tf_op jit(solution)/shard_map/ppermute | solution.py:637
  114.5 1.5 %collective-permute-start.19 = (bf16[48,1280]{1,0:T(8,128)(2,1)S(1)}, bf16[48,1280]{1,0:T(8,128)(2,1)S(1)}, u32[]{:S(2)}, u32[]{:S(2)}) collective-permute-start(bf16[48,1280]{1,0:T(8,128)(2,1)S(1)} %get-tuple-element.122), channel_id=1, source_target_pairs={{0,16},{4,20},{8,24},{12,28},{16,0},{20,4},{24,8},{28,12},{1,17},{... | collective-permute-start | bytes 368648 | tf_op jit(solution)/shard_map/ppermute | solution.py:637
  116.5 4.1 %layer_output.5.refs_3_ = bf16[12,256,384]{2,1,0:T(8,128)(2,1)} custom-call(bf16[6,1536,512]{2,1,0:T(8,128)(2,1)} %get-tuple-element.124.refs_0_, f32[6,384,512]{2,1,0:T(8,128)} %get-tuple-element.91.refs_1_, bf16[384,1536]{1,0:T(8,128)(2,1)S(1)} %get-tuple-element.92.refs_2_, bf16[12,256,384]{2,1,0:T(8,128)(2,1)} %layer_output.4.refs_3_), custom_call_target="tpu_custom_call", output_to_operand_aliasing={{}: (3, {})} | custom-call | tf_op jit(solution)/shard_map/layer_output/pallas_call | solution.py:535
  120.6 1.4 %collective-permute-done.19.refs_2_ = bf16[48,1280]{1,0:T(8,128)(2,1)S(1)} collective-permute-done((bf16[48,1280]{1,0:T(8,128)(2,1)S(1)}, bf16[48,1280]{1,0:T(8,128)(2,1)S(1)}, u32[]{:S(2)}, u32[]{:S(2)}) %collective-permute-start.19) | collective-permute-done | bytes 122912 | tf_op jit(solution)/shard_map/ppermute | solution.py:637
  122.1 1.1 collective-permute-start.22
  123.3 1.4 %collective-permute-start.21 = (bf16[48,1152]{1,0:T(8,128)(2,1)S(1)}, bf16[48,1152]{1,0:T(8,128)(2,1)S(1)}, u32[]{:S(2)}, u32[]{:S(2)}) collective-permute-start(bf16[48,1152]{1,0:T(8,128)(2,1)S(1)} %pad_maximum_fusion.1), channel_id=1, source_target_pairs={{0,2},{1,3},{2,0},{3,1},{4,6},{5,7},{6,4},{7,5},{8,10},{9,11},{10,... | collective-permute-start | bytes 331784 | tf_op jit(solution)/shard_map/ppermute | solution.py:637
  124.7 3.2 %layer_output.6.refs_3_ = bf16[12,256,384]{2,1,0:T(8,128)(2,1)} custom-call(bf16[6,1536,512]{2,1,0:T(8,128)(2,1)} %get-tuple-element.124.refs_0_, f32[6,384,512]{2,1,0:T(8,128)} %get-tuple-element.91.refs_1_, bf16[384,1536]{1,0:T(8,128)(2,1)S(1)} %get-tuple-element.92.refs_2_, bf16[12,256,384]{2,1,0:T(8,128)(2,1)} %layer_output.5.refs_3_), custom_call_target="tpu_custom_call", output_to_operand_aliasing={{}: (3, {})} | custom-call | tf_op jit(solution)/shard_map/layer_output/pallas_call | solution.py:535
  127.9 0.8 collective-permute-done.22.refs_1_
  128.8 0.9 collective-permute-start.23
  129.6 4.1 %layer_output.7 = bf16[12,256,384]{2,1,0:T(8,128)(2,1)} custom-call(bf16[6,1536,512]{2,1,0:T(8,128)(2,1)} %get-tuple-element.124.refs_0_, f32[6,384,512]{2,1,0:T(8,128)} %get-tuple-element.91.refs_1_, bf16[384,1536]{1,0:T(8,128)(2,1)S(1)} %get-tuple-element.92.refs_2_, bf16[12,256,384]{2,1,0:T(8,128)(2,1)} %layer_output.6.refs_3_), custom_call_target="tpu_custom_call", output_to_operand_aliasing={{}: (3, {})} | custom-call | tf_op jit(solution)/shard_map/layer_output/pallas_call | solution.py:535
  133.7 0.7 slice_add_fusion
  134.4 1.1 collective-permute-done.23.refs_1_
  135.5 0.7 add_last.1
  (54 shorter events, 4.0 us)
Async XLA Ops:
  0.6 16.0 %copy-start = (bf16[48,384]{1,0:T(8,128)(2,1)S(1)}, bf16[48,384]{1,0:T(8,128)(2,1)}, u32[]{:S(2)}) copy-start(bf16[48,384]{1,0:T(8,128)(2,1)} %param.17) | copy-start | bytes 110596
  1.7 14.9 %collective-permute-start.2 = (bf16[96,384]{1,0:T(8,128)(2,1)S(1)}, bf16[96,384]{1,0:T(8,128)(2,1)S(1)}, u32[]{:S(2)}, u32[]{:S(2)}) collective-permute-start(bf16[96,384]{1,0:T(8,128)(2,1)S(1)} %get-tuple-element.78), channel_id=1, source_target_pairs={{0,3},{1,2},{2,1},{3,0},{4,7},{5,6},{6,5},{7,4},{8,11},{9,10},{10,... | collective-permute-start | bytes 221192 | tf_op jit(solution)/shard_map/ppermute | solution.py:637
  6.8 6.2 %collective-permute-start.1 = (bf16[96,384]{1,0:T(8,128)(2,1)S(1)}, bf16[96,384]{1,0:T(8,128)(2,1)S(1)}, u32[]{:S(2)}, u32[]{:S(2)}) collective-permute-start(bf16[96,384]{1,0:T(8,128)(2,1)S(1)} %get-tuple-element.78), channel_id=1, source_target_pairs={{0,2},{1,3},{2,0},{3,1},{4,6},{5,7},{6,4},{7,5},{8,10},{9,11},{10,... | collective-permute-start | bytes 221192 | tf_op jit(solution)/shard_map/ppermute | solution.py:637
  6.8 4.7 %collective-permute-start = (bf16[96,384]{1,0:T(8,128)(2,1)S(1)}, bf16[96,384]{1,0:T(8,128)(2,1)S(1)}, u32[]{:S(2)}, u32[]{:S(2)}) collective-permute-start(bf16[96,384]{1,0:T(8,128)(2,1)S(1)} %get-tuple-element.78), channel_id=1, source_target_pairs={{0,1},{1,0},{2,3},{3,2},{4,5},{5,4},{6,7},{7,6},{8,9},{9,8},{10,11... | collective-permute-start | bytes 221192 | tf_op jit(solution)/shard_map/ppermute | solution.py:637
  7.5 9.0 %collective-permute-start.8 = (bf16[48,1280]{1,0:T(8,128)(2,1)S(1)}, bf16[48,1280]{1,0:T(8,128)(2,1)S(1)}, u32[]{:S(2)}, u32[]{:S(2)}) collective-permute-start(bf16[48,1280]{1,0:T(8,128)(2,1)S(1)} %get-tuple-element.79), channel_id=1, source_target_pairs={{0,24},{4,28},{8,16},{12,20},{16,8},{20,12},{24,0},{28,4},{1,25},{... | collective-permute-start | bytes 368648 | tf_op jit(solution)/shard_map/ppermute | solution.py:637
  10.1 6.4 %collective-permute-start.7 = (bf16[48,1280]{1,0:T(8,128)(2,1)S(1)}, bf16[48,1280]{1,0:T(8,128)(2,1)S(1)}, u32[]{:S(2)}, u32[]{:S(2)}) collective-permute-start(bf16[48,1280]{1,0:T(8,128)(2,1)S(1)} %get-tuple-element.79), channel_id=1, source_target_pairs={{0,16},{4,20},{8,24},{12,28},{16,0},{20,4},{24,8},{28,12},{1,17},{... | collective-permute-start | bytes 368648 | tf_op jit(solution)/shard_map/ppermute | solution.py:637
  11.6 4.9 %collective-permute-start.6 = (bf16[48,1280]{1,0:T(8,128)(2,1)S(1)}, bf16[48,1280]{1,0:T(8,128)(2,1)S(1)}, u32[]{:S(2)}, u32[]{:S(2)}) collective-permute-start(bf16[48,1280]{1,0:T(8,128)(2,1)S(1)} %get-tuple-element.79), channel_id=1, source_target_pairs={{0,8},{4,12},{8,0},{12,4},{16,24},{20,28},{24,16},{28,20},{1,9},{5... | collective-permute-start | bytes 368648 | tf_op jit(solution)/shard_map/ppermute | solution.py:637
  16.5 3.8 %collective-permute-start.9 = (bf16[192,1280]{1,0:T(8,128)(2,1)S(1)}, bf16[192,1280]{1,0:T(8,128)(2,1)S(1)}, u32[]{:S(2)}, u32[]{:S(2)}) collective-permute-start(bf16[192,1280]{1,0:T(8,128)(2,1)S(1)} %constant_dynamic-update-slice_fusion.5.refs_0_), channel_id=1, source_target_pairs={{0,4},{4,0},{8,12},{12,8},{16,20},{20,16},{24,28},{28,24},{1,5},{5... | collective-permute-start | bytes 1474568 | tf_op jit(solution)/shard_map/ppermute | solution.py:637
  16.7 21.8 %collective-permute-start.5 = (bf16[432,384]{1,0:T(8,128)(2,1)S(1)}, bf16[432,384]{1,0:T(8,128)(2,1)S(1)}, u32[]{:S(2)}, u32[]{:S(2)}) collective-permute-start(bf16[432,384]{1,0:T(8,128)(2,1)S(1)} %constant_dynamic-update-slice_fusion), channel_id=1, source_target_pairs={{0,24},{4,28},{8,16},{12,20},{16,8},{20,12},{24,0},{28,4},{1,25},{... | collective-permute-start | bytes 995336 | tf_op jit(solution)/shard_map/ppermute | solution.py:637
  19.2 19.3 %collective-permute-start.4 = (bf16[432,384]{1,0:T(8,128)(2,1)S(1)}, bf16[432,384]{1,0:T(8,128)(2,1)S(1)}, u32[]{:S(2)}, u32[]{:S(2)}) collective-permute-start(bf16[432,384]{1,0:T(8,128)(2,1)S(1)} %constant_dynamic-update-slice_fusion), channel_id=1, source_target_pairs={{0,16},{4,20},{8,24},{12,28},{16,0},{20,4},{24,8},{28,12},{1,17},{... | collective-permute-start | bytes 995336 | tf_op jit(solution)/shard_map/ppermute | solution.py:637
  19.7 18.8 %collective-permute-start.3 = (bf16[432,384]{1,0:T(8,128)(2,1)S(1)}, bf16[432,384]{1,0:T(8,128)(2,1)S(1)}, u32[]{:S(2)}, u32[]{:S(2)}) collective-permute-start(bf16[432,384]{1,0:T(8,128)(2,1)S(1)} %constant_dynamic-update-slice_fusion), channel_id=1, source_target_pairs={{0,8},{4,12},{8,0},{12,4},{16,24},{20,28},{24,16},{28,20},{1,9},{5... | collective-permute-start | bytes 995336 | tf_op jit(solution)/shard_map/ppermute | solution.py:637
  38.8 3.1 %collective-permute-start.10 = (bf16[1728,384]{1,0:T(8,128)(2,1)S(1)}, bf16[1728,384]{1,0:T(8,128)(2,1)S(1)}, u32[]{:S(2)}, u32[]{:S(2)}) collective-permute-start(bf16[1728,384]{1,0:T(8,128)(2,1)S(1)} %constant_dynamic-update-slice_fusion.9.refs_0_), channel_id=1, source_target_pairs={{0,4},{4,0},{8,12},{12,8},{16,20},{20,16},{24,28},{28,24},{1,5},{5... | collective-permute-start | bytes 3981320 | tf_op jit(solution)/shard_map/ppermute | solution.py:637
  77.4 3.4 %collective-permute-start.11 = (bf16[4,48,3456]{2,1,0:T(8,128)(2,1)S(1)}, bf16[4,48,3456]{2,1,0:T(8,128)(2,1)S(1)}, u32[]{:S(2)}, u32[]{:S(2)}) collective-permute-start(bf16[4,48,3456]{2,1,0:T(8,128)(2,1)S(1)} %get-tuple-element.89), channel_id=1, source_target_pairs={{0,4},{4,0},{8,12},{12,8},{16,20},{20,16},{24,28},{28,24},{1,5},{5... | collective-permute-start | bytes 3981320 | tf_op jit(solution)/shard_map/ppermute | solution.py:637
  81.2 27.2 %collective-permute-start.12 = (bf16[48,3456]{1,0:T(8,128)(2,1)S(1)}, bf16[48,3456]{1,0:T(8,128)(2,1)S(1)}, u32[]{:S(2)}, u32[]{:S(2)}) collective-permute-start(bf16[48,3456]{1,0:T(8,128)(2,1)S(1)} %get-tuple-element.97), channel_id=1, source_target_pairs={{0,8},{4,12},{8,0},{12,4},{16,24},{20,28},{24,16},{28,20},{1,9},{5... | collective-permute-start | bytes 995336 | tf_op jit(solution)/shard_map/ppermute | solution.py:637
  82.7 25.6 %collective-permute-start.13 = (bf16[48,3456]{1,0:T(8,128)(2,1)S(1)}, bf16[48,3456]{1,0:T(8,128)(2,1)S(1)}, u32[]{:S(2)}, u32[]{:S(2)}) collective-permute-start(bf16[48,3456]{1,0:T(8,128)(2,1)S(1)} %get-tuple-element.98), channel_id=1, source_target_pairs={{0,16},{4,20},{8,24},{12,28},{16,0},{20,4},{24,8},{28,12},{1,17},{... | collective-permute-start | bytes 995336 | tf_op jit(solution)/shard_map/ppermute | solution.py:637
  84.3 24.1 %collective-permute-start.14 = (bf16[48,3456]{1,0:T(8,128)(2,1)S(1)}, bf16[48,3456]{1,0:T(8,128)(2,1)S(1)}, u32[]{:S(2)}, u32[]{:S(2)}) collective-permute-start(bf16[48,3456]{1,0:T(8,128)(2,1)S(1)} %get-tuple-element.99), channel_id=1, source_target_pairs={{0,24},{4,28},{8,16},{12,20},{16,8},{20,12},{24,0},{28,4},{1,25},{... | collective-permute-start | bytes 995336 | tf_op jit(solution)/shard_map/ppermute | solution.py:637
  108.4 1.2 collective-permute-start.15
  108.5 3.8 %collective-permute-start.17 = (bf16[4,48,1152]{2,1,0:T(8,128)(2,1)S(1)}, bf16[4,48,1152]{2,1,0:T(8,128)(2,1)S(1)}, u32[]{:S(2)}, u32[]{:S(2)}) collective-permute-start(bf16[4,48,1152]{2,1,0:T(8,128)(2,1)S(1)} %get-tuple-element.116), channel_id=1, source_target_pairs={{0,4},{4,0},{8,12},{12,8},{16,20},{20,16},{24,28},{28,24},{1,5},{5... | collective-permute-start | bytes 1327112 | tf_op jit(solution)/shard_map/ppermute | solution.py:637
  109.7 13.6 %collective-permute-start.16 = (bf16[48,1920]{1,0:T(8,128)(2,1)S(1)}, bf16[48,1920]{1,0:T(8,128)(2,1)S(1)}, u32[]{:S(2)}, u32[]{:S(2)}) collective-permute-start(bf16[48,1920]{1,0:T(8,128)(2,1)S(1)} %pad_maximum_fusion), channel_id=1, source_target_pairs={{0,1},{1,0},{2,3},{3,2},{4,5},{5,4},{6,7},{7,6},{8,9},{9,8},{10,11... | collective-permute-start | bytes 552968 | tf_op jit(solution)/shard_map/ppermute | solution.py:637
  113.0 7.6 %collective-permute-start.18 = (bf16[48,1280]{1,0:T(8,128)(2,1)S(1)}, bf16[48,1280]{1,0:T(8,128)(2,1)S(1)}, u32[]{:S(2)}, u32[]{:S(2)}) collective-permute-start(bf16[48,1280]{1,0:T(8,128)(2,1)S(1)} %get-tuple-element.121), channel_id=1, source_target_pairs={{0,8},{4,12},{8,0},{12,4},{16,24},{20,28},{24,16},{28,20},{1,9},{5... | collective-permute-start | bytes 368648 | tf_op jit(solution)/shard_map/ppermute | solution.py:637
  114.5 7.5 %collective-permute-start.19 = (bf16[48,1280]{1,0:T(8,128)(2,1)S(1)}, bf16[48,1280]{1,0:T(8,128)(2,1)S(1)}, u32[]{:S(2)}, u32[]{:S(2)}) collective-permute-start(bf16[48,1280]{1,0:T(8,128)(2,1)S(1)} %get-tuple-element.122), channel_id=1, source_target_pairs={{0,16},{4,20},{8,24},{12,28},{16,0},{20,4},{24,8},{28,12},{1,17},{... | collective-permute-start | bytes 368648 | tf_op jit(solution)/shard_map/ppermute | solution.py:637
  116.1 6.0 %collective-permute-start.20 = (bf16[48,1280]{1,0:T(8,128)(2,1)S(1)}, bf16[48,1280]{1,0:T(8,128)(2,1)S(1)}, u32[]{:S(2)}, u32[]{:S(2)}) collective-permute-start(bf16[48,1280]{1,0:T(8,128)(2,1)S(1)} %get-tuple-element.123), channel_id=1, source_target_pairs={{0,24},{4,28},{8,16},{12,20},{16,8},{20,12},{24,0},{28,4},{1,25},{... | collective-permute-start | bytes 368648 | tf_op jit(solution)/shard_map/ppermute | solution.py:637
  122.1 6.6 %collective-permute-start.22 = (bf16[48,1280]{1,0:T(8,128)(2,1)S(1)}, bf16[48,1280]{1,0:T(8,128)(2,1)S(1)}, u32[]{:S(2)}, u32[]{:S(2)}) collective-permute-start(bf16[48,1280]{1,0:T(8,128)(2,1)S(1)} %add_plane.1.refs_0_), channel_id=1, source_target_pairs={{0,1},{1,0},{2,3},{3,2},{4,5},{5,4},{6,7},{7,6},{8,9},{9,8},{10,11... | collective-permute-start | bytes 368648 | tf_op jit(solution)/shard_map/ppermute | solution.py:637
  123.3 10.4 %collective-permute-start.21 = (bf16[48,1152]{1,0:T(8,128)(2,1)S(1)}, bf16[48,1152]{1,0:T(8,128)(2,1)S(1)}, u32[]{:S(2)}, u32[]{:S(2)}) collective-permute-start(bf16[48,1152]{1,0:T(8,128)(2,1)S(1)} %pad_maximum_fusion.1), channel_id=1, source_target_pairs={{0,2},{1,3},{2,0},{3,1},{4,6},{5,7},{6,4},{7,5},{8,10},{9,11},{10,... | collective-permute-start | bytes 331784 | tf_op jit(solution)/shard_map/ppermute | solution.py:637
  128.8 6.8 %collective-permute-start.23 = (bf16[48,1280]{1,0:T(8,128)(2,1)S(1)}, bf16[48,1280]{1,0:T(8,128)(2,1)S(1)}, u32[]{:S(2)}, u32[]{:S(2)}) collective-permute-start(bf16[48,1280]{1,0:T(8,128)(2,1)S(1)} %add_near.1.refs_0_), channel_id=1, source_target_pairs={{0,2},{1,3},{2,0},{3,1},{4,6},{5,7},{6,4},{7,5},{8,10},{9,11},{10,... | collective-permute-start | bytes 368648 | tf_op jit(solution)/shard_map/ppermute | solution.py:637
